TPU v7x, 32 devices: a whole 2x2x4 slice. The times are simulated.
32 devices in a mesh: grp: 2 (over x), dp: 4 (over z), mp: 4 (over y, core).
Axes of the slice: x: 2, y: 2, z: 4, core: 2. Of those that a mesh axis runs over, the one named last changes fastest.
Arguments:
- captured: bfloat16 [3, 256, 8192], P(None, 'mp', ('grp', 'dp')), may hold values from -9 to 9
- unite_weight: bfloat16 [3, 8192, 8192], P(None, ('grp', 'dp'), 'mp'), may hold values from -0.0390625 to 0.0390625
- heads: bfloat16 [2, 16000, 8192], P('grp', 'dp', 'mp'), may hold values from -10 to 10, as said below
- final_hidden: bfloat16 [256, 8192], P('dp', 'mp'), may hold values from -9 to 9
- target_gain: float32 [8192], P('mp'), may hold values from 0.1 to 1.9
- draft_gain: float32 [8192], P('mp'), may hold values from 0.1 to 1.9
- lengths: int32 [4], replicated, may hold values from 32 to 64
Outputs:
- grad_terms: bfloat16 [2, 16000, 8192], P('grp', 'dp', 'mp')
- token_loss: float32 [256], P('mp')
Inputs may be any that keep to these rules, and one draw needn't show every extreme that they name: `heads`: each row of a head has its own scale.
All inputs are finite; a program needn't handle non-finite values.
Results may differ from a plain program's by a relative error of at most 0.0051.
Values may be sent and summed in bfloat16 or wider, within the bound.
A program may use at most 128 MiB of HBM per device.

v0:
```python
import jax
import jax.numpy as jnp
from jax import lax
from jax.sharding import PartitionSpec as P

EPSILON = 1e-05


def merged(shard, axis, combine):
    everything = jax.tree.map(lambda part: lax.all_gather(part, axis), shard)
    leading = jax.tree.map(lambda part: part[0], everything)

    def lap(k, so_far):
        return combine(so_far, jax.tree.map(lambda part: part[k], everything))

    return lax.fori_loop(1, lax.axis_size(axis), lap, leading)


def partner(shard, axis, stride):
    return lax.ppermute(shard, axis, [(i, i ^ 1 << stride) for i in range(lax.axis_size(axis))])


def per_device(captured, unite_weight, heads, final_hidden, target_gain, draft_gain, lengths):
    model_width = final_hidden.shape[1] * lax.axis_size("mp")
    slab_length = final_hidden.shape[0]
    is_target = lax.axis_index("grp") == 0
    head_rows = heads[0]
    segment = lax.all_gather(captured, "mp", axis=1, tiled=True)
    running = jnp.dot(segment[0], unite_weight[0], preferred_element_type=jnp.float32)
    for layer_index in range(1, segment.shape[0]):
        running = running + jnp.dot(
            segment[layer_index], unite_weight[layer_index], preferred_element_type=jnp.float32
        )
    united = lax.psum(running, ("grp", "dp"))
    last_values = lax.all_gather(final_hidden, "dp", axis=0, tiled=True).astype(jnp.float32)
    square_sums = lax.psum(
        (jnp.sum(united * united, axis=1), jnp.sum(last_values * last_values, axis=1)), "mp"
    )
    draft_scale = lax.rsqrt(square_sums[0] / model_width + EPSILON)
    target_scale = lax.rsqrt(square_sums[1] / model_width + EPSILON)
    draft_rows = (united * draft_scale[:, None] * draft_gain[None, :]).astype(jnp.bfloat16)
    target_rows = (last_values * target_scale[:, None] * target_gain[None, :]).astype(jnp.bfloat16)
    own_rows = jnp.where(is_target, target_rows, draft_rows)
    row_share = own_rows.shape[0] // lax.axis_size("mp")
    logits = lax.psum_scatter(
        jnp.einsum("td,vd->tv", own_rows, head_rows, preferred_element_type=jnp.float32),
        "mp",
        scatter_dimension=0,
        tiled=True,
    )
    local_max = jnp.max(logits, axis=1)
    local_total = jnp.sum(jnp.exp(logits - local_max[:, None]), axis=1)

    def combine(first_pair, second_pair):
        joined_max = jnp.maximum(first_pair[0], second_pair[0])
        joined_total = first_pair[1] * jnp.exp(first_pair[0] - joined_max) + second_pair[
            1
        ] * jnp.exp(second_pair[0] - joined_max)
        return (joined_max, joined_total)

    row_max, row_total = merged((local_max, local_total), "dp", combine)
    shifted = logits - row_max[:, None]
    probabilities = jnp.exp(shifted) / row_total[:, None]
    log_probs = shifted - jnp.log(row_total)[:, None]
    outgoing = jnp.where(is_target, probabilities, log_probs)
    incoming = partner(outgoing, "grp", 0)
    target_probs = jnp.where(is_target, probabilities, incoming)
    draft_logs = jnp.where(is_target, incoming, log_probs)
    token_index = lax.axis_index("mp") * row_share + lax.iota(jnp.int32, row_share)
    slab_index = token_index // slab_length
    position = token_index - slab_index * slab_length
    matches = slab_index[:, None] == lax.iota(jnp.int32, lengths.shape[0])[None, :]
    valid_len = jnp.sum(jnp.where(matches, lengths[None, :], 0), axis=1)
    valid_mask = (position < valid_len).astype(jnp.float32)
    valid_total = jnp.sum(lengths).astype(jnp.float32)
    cross_term = lax.psum(jnp.sum(target_probs * draft_logs, axis=1), "dp")
    token_loss = -valid_mask * cross_term
    mixed = jnp.where(is_target, probabilities, probabilities - target_probs)
    weighted = (mixed * (valid_mask / valid_total)[:, None]).astype(jnp.bfloat16)
    summed = jnp.einsum(
        "tv,td->vd",
        lax.all_gather(weighted, "mp", axis=0, tiled=True),
        draft_rows,
        preferred_element_type=jnp.float32,
    )
    sign_factor = jnp.where(is_target, -1.0, 1.0).astype(jnp.float32)
    grad_terms = (sign_factor * summed).astype(jnp.bfloat16)[None]
    return (grad_terms, token_loss)


def solution(mesh):
    in_specs = (
        P(None, "mp", ("grp", "dp")),
        P(None, ("grp", "dp"), "mp"),
        P("grp", "dp", "mp"),
        P("dp", "mp"),
        P("mp"),
        P("mp"),
        P(),
    )
    out_specs = (P("grp", "dp", "mp"), P("mp"))
    return jax.shard_map(
        per_device, mesh=mesh, in_specs=in_specs, out_specs=out_specs, check_vma=False
    )
```

profile of v0, /device:TPU:0, one launch (start us, length us, event | category | flops | bytes accessed | tf_op | source)
XLA Modules:
  0.0 316.7 jit_solution(6157457129729815724)
XLA Ops:
  7.2 0.0 all-gather.8.cloned.1.call-start
  7.2 0.7 all-gather.8.cloned.1.call-update
  7.9 0.0 all-gather.6.cloned.1.call-start
  7.9 0.7 all-gather.6.cloned.1.call-update
  8.6 0.0 all-reduce.6.cloned.1.call-start
  8.7 23.3 %all-gather.8.cloned.1.call-done = bf16[3,256,1024]{2,1,0:T(8,128)(2,1)} async-done(((bf16[3,64,1024]{2,1,0:T(8,128)(2,1)}), bf16[3,256,1024]{2,1,0:T(8,128)(2,1)}) %all-gather.8.cloned.1.call-update) | async-done | bytes 1572880 | tf_op jit(solution)/shard_map/all_gather | solution.py:28
  32.0 0.0 copy-start.3
  32.0 3.7 %fusion.7 = f32[256,2048]{1,0:T(8,128)S(1)} fusion(bf16[3,1024,2048]{2,1,0:T(8,128)(2,1)} %param.10, bf16[3,256,1024]{2,1,0:T(8,128)(2,1)} %all-gather.8.cloned.1.call-done), kind=kOutput, calls=%fused_computation.12 | convolution fusion | flops 1073741824 | bytes 6815744 | tf_op jit(solution)/shard_map/dot_general | solution.py:31
  35.7 0.0 copy-done.3
  35.7 3.5 %fusion.14 = f32[256,2048]{1,0:T(8,128)S(1)} fusion(f32[256,2048]{1,0:T(8,128)S(1)} %fusion.7, bf16[3,1024,2048]{2,1,0:T(8,128)(2,1)} %param.10, bf16[3,256,1024]{2,1,0:T(8,128)(2,1)S(1)} %copy-done.3), kind=kOutput, calls=%fused_computation.19 | convolution fusion | flops 1074266112 | bytes 8912896 | tf_op jit(solution)/shard_map/dot_general | solution.py:29
  39.2 4.9 %fusion.17 = f32[256,2048]{1,0:T(8,128)} fusion(f32[256,2048]{1,0:T(8,128)S(1)} %fusion.14, bf16[3,1024,2048]{2,1,0:T(8,128)(2,1)} %param.10, bf16[3,256,1024]{2,1,0:T(8,128)(2,1)S(1)} %copy-done.3), kind=kOutput, calls=%fused_computation.20 | convolution fusion | flops 1074266112 | bytes 8912896 | tf_op jit(solution)/shard_map/dot_general | solution.py:31
  44.1 0.0 all-reduce.6.cloned.1.call-update
  44.2 0.0 copy-start.4
  44.2 0.0 copy-start.5
  44.2 0.0 reduce-scatter.2.cloned.1.call-start
  44.3 17.2 %all-gather.6.cloned.1.call-done = bf16[256,2048]{1,0:T(8,128)(2,1)} async-done(((bf16[64,2048]{1,0:T(8,128)(2,1)}), bf16[256,2048]{1,0:T(8,128)(2,1)}) %all-gather.6.cloned.1.call-update) | async-done | bytes 1048592 | tf_op jit(solution)/shard_map/all_gather | solution.py:35
  61.5 0.0 copy-start.2
  61.5 1.6 fusion.20
  63.1 104.0 %all-reduce.6.cloned.1.call-done = f32[256,2048]{1,0:T(8,128)} async-done(((f32[256,2048]{1,0:T(8,128)}), f32[256,2048]{1,0:T(8,128)}) %all-reduce.6.cloned.1.call-update) | async-done | bytes 2097168 | tf_op jit(solution)/shard_map/psum | solution.py:34
  167.1 0.0 copy-start.1
  167.1 2.0 multiply_reduce_fusion
  169.0 6.3 %all-reduce.2 = (f32[256]{0:T(256)S(1)}, f32[256]{0:T(256)S(1)}) all-reduce(f32[256]{0:T(256)S(1)} %fusion.20, f32[256]{0:T(256)S(1)} %multiply_reduce_fusion), channel_id=1, replica_groups=mesh['grp'=2,'dp'=4,'mp'=4] {'mp'}, use_global_device_ids=true, to_apply=%region_1.0 | all-reduce | flops 512 | bytes 4096 | tf_op jit(solution)/shard_map/psum | solution.py:36
  175.4 0.0 copy-done.4
  175.4 0.0 copy-done.5
  175.4 0.0 copy-done.2
  175.4 0.0 copy-done.1
  175.4 18.1 %fusion.3 = f32[256,4000]{1,0:T(8,128)} fusion(bf16[1,4000,2048]{2,1,0:T(8,128)(2,1)} %param.11, bf16[256,2048]{1,0:T(8,128)(2,1)S(1)} %copy-done.2, f32[2048]{0:T(1024)S(1)} %copy-done.4, f32[256]{0:T(256)S(1)} %get-tuple-element.156, pred[]{:T(512)S(6)} %eq.16, f32[256,2048]{1,0:T(8,128)S(1)} %copy-done.1, f32[2048]{0:T(1024)S(1)} %copy-done.5, ...), kind=kOutput, calls=%fused_computation.8 | convolution fusion | flops 4198498304 | bytes 23644160 | tf_op jit(solution)/shard_map/td,vd->tv/dot_general | solution.py:46
  193.5 0.0 copy-start.7
  193.5 0.0 reduce-scatter.2.cloned.1.call-update
  193.5 0.0 all-gather.10.cloned.1.call-start
  193.6 0.6 copy-done.7
  194.1 0.7 dynamic-slice
  195.5 0.0 copy-start.6
  195.5 42.0 %reduce-scatter.2.cloned.1.call-done = f32[64,4000]{1,0:T(8,128)} async-done(((f32[256,4000]{1,0:T(8,128)}), f32[64,4000]{1,0:T(8,128)}) %reduce-scatter.2.cloned.1.call-update) | async-done | bytes 1024016 | tf_op jit(solution)/shard_map/reduce_scatter | solution.py:45
  237.5 0.0 copy-start
  237.5 1.5 reduce_max.9
  239.0 0.2 dynamic-update-slice
  239.2 1.5 exponential_reduce_fusion
  240.8 0.2 dynamic-update-slice.1
  241.0 11.7 %all-reduce.3 = (f32[256]{0:T(256)S(1)}, f32[256]{0:T(256)S(1)}) all-reduce(f32[256]{0:T(256)S(1)} %dynamic-update-slice, f32[256]{0:T(256)S(1)} %dynamic-update-slice.1), channel_id=2, replica_groups=mesh['grp'=2,'dp'=4,'mp'=4] {'dp'}, use_global_device_ids=true, to_apply=%add | all-reduce | flops 512 | bytes 4096
  252.7 0.1 reshape.41
  252.8 0.1 reshape.40
  252.9 0.1 while.17
  253.0 0.0 copy-done
  253.0 1.3 subtract_select_fusion.1
  254.3 1.5 collective-permute-start
  255.7 0.0 copy-done.6
  255.7 0.6 reduce_sum.58
  257.1 0.1 select_reduce_fusion
  257.2 20.3 %collective-permute-done = f32[64,4000]{1,0:T(8,128)} collective-permute-done((f32[64,4000]{1,0:T(8,128)}, f32[64,4000]{1,0:T(8,128)}, u32[]{:S(2)}, u32[]{:S(2)}) %collective-permute-start) | collective-permute-done | bytes 1024032 | tf_op jit(solution)/shard_map/ppermute | solution.py:20
  277.5 2.6 multiply_reduce_fusion.1
  280.1 0.0 all-gather.10.cloned.1.call-update
  280.2 8.4 %psum.31 = f32[64]{0:T(128)S(1)} all-reduce(f32[64]{0:T(128)S(1)} %get-tuple-element.153), channel_id=1, replica_groups=mesh['grp'=2,'dp'=4,'mp'=4] {'dp'}, use_global_device_ids=true, to_apply=%region_13.14 | all-reduce | flops 64 | bytes 512 | tf_op jit(solution)/shard_map/psum | solution.py:76
  288.6 0.5 negate_multiply_fusion
  289.1 11.0 %all-gather.10.cloned.1.call-done = bf16[256,4000]{1,0:T(8,128)(2,1)} async-done(((bf16[64,4000]{1,0:T(8,128)(2,1)}), bf16[256,4000]{1,0:T(8,128)(2,1)}) %all-gather.10.cloned.1.call-update) | async-done | bytes 2048016 | tf_op jit(solution)/shard_map/all_gather | solution.py:82
  300.1 10.0 %fusion.2 = bf16[1,4000,2048]{2,1,0:T(8,128)(2,1)} fusion(f32[]{:T(128)S(6)} %select_n.59, bf16[256,4000]{1,0:T(8,128)(2,1)} %all-gather.10.cloned.1.call-done, f32[256,2048]{1,0:T(8,128)S(1)} %copy-done.1, f32[2048]{0:T(1024)S(1)} %copy-done.5, f32[256]{0:T(256)S(1)} %get-tuple-element.155), kind=kOutput, calls=%fused_computation.7 | convolution fusion | flops 4212260864 | bytes 20538372 | tf_op jit(solution)/shard_map/tv,td->vd/dot_general | solution.py:80
  (11 shorter events, 0.1 us)
Async XLA Ops:
  7.2 24.8 %all-gather.8.cloned.1.call-start = ((), (), s32[]{:S(2)}) async-start(), calls=%async_computation.2 | async-start | bytes 1966080 | tf_op jit(solution)/shard_map/all_gather | solution.py:28
  7.9 53.6 %all-gather.6.cloned.1.call-start = ((), (), s32[]{:S(2)}) async-start(), calls=%async_computation.1 | async-start | bytes 1310720 | tf_op jit(solution)/shard_map/all_gather | solution.py:35
  8.6 158.4 %all-reduce.6.cloned.1.call-start = ((), (), s32[]{:S(2)}) async-start(), calls=%async_computation.3 | async-start | bytes 4194304 | tf_op jit(solution)/shard_map/psum | solution.py:34
  32.0 3.7 %copy-start.3 = (bf16[3,256,1024]{2,1,0:T(8,128)(2,1)S(1)}, bf16[3,256,1024]{2,1,0:T(8,128)(2,1)}, u32[]{:S(2)}) copy-start(bf16[3,256,1024]{2,1,0:T(8,128)(2,1)} %all-gather.8.cloned.1.call-done) | copy-start | bytes 4718596
  44.2 131.2 %copy-start.4 = (f32[2048]{0:T(1024)S(1)}, f32[2048]{0:T(1024)}, u32[]{:S(2)}) copy-start(f32[2048]{0:T(1024)} %param.13) | copy-start | bytes 24580
  44.2 131.2 %copy-start.5 = (f32[2048]{0:T(1024)S(1)}, f32[2048]{0:T(1024)}, u32[]{:S(2)}) copy-start(f32[2048]{0:T(1024)} %param.14) | copy-start | bytes 24580
  44.2 193.3 %reduce-scatter.2.cloned.1.call-start = ((), (), s32[]{:S(2)}) async-start(), calls=%async_computation.4 | async-start | bytes 5242880 | tf_op jit(solution)/shard_map/reduce_scatter | solution.py:45
  61.5 113.9 %copy-start.2 = (bf16[256,2048]{1,0:T(8,128)(2,1)S(1)}, bf16[256,2048]{1,0:T(8,128)(2,1)}, u32[]{:S(2)}) copy-start(bf16[256,2048]{1,0:T(8,128)(2,1)} %all-gather.6.cloned.1.call-done) | copy-start | bytes 3145732
  167.1 8.3 %copy-start.1 = (f32[256,2048]{1,0:T(8,128)S(1)}, f32[256,2048]{1,0:T(8,128)}, u32[]{:S(2)}) copy-start(f32[256,2048]{1,0:T(8,128)} %all-reduce.6.cloned.1.call-done) | copy-start | bytes 6291460
  193.5 0.7 copy-start.7
  193.5 106.6 %all-gather.10.cloned.1.call-start = ((), (), s32[]{:S(2)}) async-start(), calls=%async_computation.5 | async-start | bytes 2621440 | tf_op jit(solution)/shard_map/all_gather | solution.py:82
  195.5 60.3 %copy-start.6 = (s32[4]{0:T(128)S(1)}, s32[4]{0:T(128)}, u32[]{:S(2)}) copy-start(s32[4]{0:T(128)} %param.15) | copy-start | bytes 52
  237.5 15.5 %copy-start = (f32[64,4000]{1,0:T(8,128)S(1)}, f32[64,4000]{1,0:T(8,128)}, u32[]{:S(2)}) copy-start(f32[64,4000]{1,0:T(8,128)} %reduce-scatter.2.cloned.1.call-done) | copy-start | bytes 3072004
  254.3 23.2 %collective-permute-start = (f32[64,4000]{1,0:T(8,128)}, f32[64,4000]{1,0:T(8,128)}, u32[]{:S(2)}, u32[]{:S(2)}) collective-permute-start(f32[64,4000]{1,0:T(8,128)} %subtract_select_fusion.1), channel_id=1, source_target_pairs={{0,16},{16,0},{1,17},{17,1},{2,18},{18,2},{3,19},{19,3},{4,20},{20... | collective-permute-start | bytes 3072008 | tf_op jit(solution)/shard_map/ppermute | solution.py:20
Sparse Core Ops, SparseCore 0:
  9.6 22.3 all-gather.7
  33.5 27.9 all-gather.5
  65.7 101.3 all-reduce.5
  193.6 43.8 reduce-scatter.1
  280.3 19.8 all-gather.9
where the time goes:
time: 317 us
  waiting for transfers between devices  219 us (69%)
  matrix products  40.3 us (13%)
  blocking collectives  26.4 us (8%)
  between operations  15.3 us (5%)
  other arithmetic  11.8 us (4%)
    psum x1, waiting for transfers between devices, per_device(): united = lax.psum(running, ('grp', 'dp'))  104 us
    reduce_scatter x1, waiting for transfers between devices, per_device(): lax.psum_scatter(jnp.einsum('td,vd->tv', own_rows, head_rows, preferred_e...  42 us
    all_gather x1, waiting for transfers between devices, per_device(): segment = lax.all_gather(captured, 'mp', axis=1, tiled=True)  23.3 us
    ppermute x1, waiting for transfers between devices, partner(): lax.ppermute(shard, axis, [(i, i ^ 1 << stride) for i in range(lax.axis_s...  20.3 us
    dot_general x1, matrix products, per_device(): jnp.einsum('td,vd->tv', own_rows, head_rows, preferred_element_type=jnp.f...  18.1 us
    all_gather x1, waiting for transfers between devices, per_device(): lax.all_gather(final_hidden, 'dp', axis=0, tiled=True).astype(jnp.float32)  17.2 us
    unnamed x1, blocking collectives  11.7 us
    all_gather x1, waiting for transfers between devices, per_device(): lax.all_gather(weighted, 'mp', axis=0, tiled=True)  11 us
  transfers between devices with their start and end apart: 6, of which 6 were waited for; matrix products, arithmetic and copies ran while one was open for 5% of the time, Pallas kernels for 0%

commit v1 on v0

v1 whole, which is shorter than its diff:
```python
import functools

import jax
import jax.numpy as jnp
from jax import lax
from jax.experimental import pallas as pl
from jax.experimental.pallas import tpu as pltpu
from jax.sharding import PartitionSpec as P

EPSILON = 1e-05
PARTIAL = jnp.bfloat16
MESH = pl.DeviceIdType.MESH


def whole_axis(axis):
    return lambda: (lax.axis_size(axis), lax.axis_index(axis), lambda p: {axis: p})


def both_axes():
    outer, inner = lax.axis_size("grp"), lax.axis_size("dp")
    me = lax.axis_index("grp") * inner + lax.axis_index("dp")
    return (outer * inner, me, lambda p: {"grp": lax.div(p, inner), "dp": lax.rem(p, inner)})


def pair():
    index = lax.axis_index("mp")
    return (2, lax.rem(index, 2), lambda p: {"mp": lax.div(index, 2) * 2 + p})


def across():
    index = lax.axis_index("mp")
    count = lax.axis_size("mp") // 2
    return (count, lax.div(index, 2), lambda p: {"mp": p * 2 + lax.rem(index, 2)})


def rows_at(ref, dim, index, size):
    window = pl.ds(pl.multiple_of(index * size, size), size)
    return ref.at[(slice(None),) * dim + (window,)]


def exchange_body(items, *refs):
    count = len(items)
    ins, outs = refs[:count], refs[count : 2 * count]
    local_sem, send_sem, recv_sem = refs[2 * count :]
    groups = [item[0]() for item in items]
    barrier = pltpu.get_barrier_semaphore()
    total = 0
    for n, me, place in groups:
        for k in range(1, n):
            pl.semaphore_signal(
                barrier, inc=1, device_id=place(lax.rem(me + k, n)), device_id_type=MESH
            )
        total += n - 1
    pl.semaphore_wait(barrier, total)
    copies = []
    slot = 0
    for number, ((_, kind, dim), (n, me, place)) in enumerate(zip(items, groups)):
        source, target = ins[number], outs[number]
        size = target.shape[dim] // n
        landing = rows_at(target, dim, me, size)
        for k in range(1, n):
            peer = lax.rem(me + k, n)
            sent = source if kind == "gather" else rows_at(source, dim, peer, size)
            copy = pltpu.make_async_remote_copy(
                src_ref=sent,
                dst_ref=landing,
                send_sem=send_sem.at[slot],
                recv_sem=recv_sem.at[slot],
                device_id=place(peer),
                device_id_type=MESH,
            )
            copy.start()
            copies.append(copy)
            slot += 1
        kept = source if kind == "gather" else rows_at(source, dim, me, size)
        own = pltpu.make_async_copy(kept, landing, local_sem.at[number])
        own.start()
        copies.append(own)
    for copy in copies:
        copy.wait()


def exchange(number, arrays, items):
    shapes = []
    slots = 0
    for array, (group, kind, dim) in zip(arrays, items):
        n = group()[0]
        slots += n - 1
        shape = list(array.shape)
        if kind == "gather":
            shape[dim] *= n
        shapes.append(jax.ShapeDtypeStruct(tuple(shape), array.dtype))
    return pl.pallas_call(
        functools.partial(exchange_body, items),
        out_shape=shapes,
        in_specs=[pl.BlockSpec(memory_space=pl.ANY)] * len(arrays),
        out_specs=[pl.BlockSpec(memory_space=pl.ANY)] * len(arrays),
        scratch_shapes=[
            pltpu.SemaphoreType.DMA((len(arrays),)),
            pltpu.SemaphoreType.DMA((slots,)),
            pltpu.SemaphoreType.DMA((slots,)),
        ],
        compiler_params=pltpu.CompilerParams(collective_id=number, has_side_effects=True),
    )(*arrays)


def as_tile(parts):
    flat = jnp.concatenate([part.reshape(-1) for part in parts])
    padded = -(-flat.shape[0] // 1024) * 1024
    return jnp.pad(flat, (0, padded - flat.shape[0])).reshape(1, -1, 128)


def per_device(captured, unite_weight, heads, final_hidden, target_gain, draft_gain, lengths):
    mp_size = lax.axis_size("mp")
    dp_size = lax.axis_size("dp")
    grp_size = lax.axis_size("grp")
    model_width = final_hidden.shape[1] * mp_size
    slab_length = final_hidden.shape[0]
    is_target = lax.axis_index("grp") == 0
    head_rows = heads[0]
    segment, last = exchange(
        1,
        (captured, final_hidden),
        ((whole_axis("mp"), "gather", 1), (whole_axis("dp"), "gather", 0)),
    )
    tokens = last.shape[0]
    running = jnp.dot(segment[0], unite_weight[0], preferred_element_type=jnp.float32)
    for layer_index in range(1, segment.shape[0]):
        running = running + jnp.dot(
            segment[layer_index], unite_weight[layer_index], preferred_element_type=jnp.float32
        )
    members = grp_size * dp_size
    (arrived,) = exchange(2, (running.astype(PARTIAL),), ((both_axes, "swap", 0),))
    share = tokens // members
    arrived = arrived.reshape(members, share, -1)
    united = jnp.sum(arrived.astype(jnp.float32), axis=0)
    last_values = last.astype(jnp.float32)
    (squares,) = exchange(
        3,
        (as_tile([jnp.sum(united * united, axis=1), jnp.sum(last_values * last_values, axis=1)]),),
        ((whole_axis("mp"), "gather", 0),),
    )
    squares = jnp.sum(squares, axis=0).reshape(-1)
    draft_scale = lax.rsqrt(squares[:share] / model_width + EPSILON)
    target_scale = lax.rsqrt(squares[share : share + tokens] / model_width + EPSILON)
    draft_part = (united * draft_scale[:, None] * draft_gain[None, :]).astype(jnp.bfloat16)
    target_rows = (last_values * target_scale[:, None] * target_gain[None, :]).astype(jnp.bfloat16)
    (draft_rows,) = exchange(4, (draft_part,), ((both_axes, "gather", 0),))
    own_rows = jnp.where(is_target, target_rows, draft_rows)
    row_share = tokens // mp_size
    partial_logits = jnp.einsum(
        "td,vd->tv", own_rows, head_rows, preferred_element_type=jnp.float32
    )
    vocab = partial_logits.shape[1]
    by_core = partial_logits.reshape(mp_size // 2, 2, row_share, vocab)
    (by_core,) = exchange(5, (by_core,), ((pair, "swap", 1),))
    by_chip = by_core[:, 0] + by_core[:, 1]
    (by_chip,) = exchange(6, (by_chip,), ((across, "swap", 0),))
    logits = jnp.sum(by_chip, axis=0)
    local_max = jnp.max(logits, axis=1)
    shifted = logits - local_max[:, None]
    raised = jnp.exp(shifted)
    local_total = jnp.sum(raised, axis=1)
    incoming = lax.ppermute(raised.astype(jnp.bfloat16), "grp", [(0, 1)]).astype(jnp.float32)
    crossed = jnp.sum(incoming * shifted, axis=1)
    incoming_total = jnp.sum(incoming, axis=1)
    (stats,) = exchange(
        7,
        (as_tile([local_max, local_total, crossed, incoming_total]),),
        ((both_axes, "gather", 0),),
    )
    stats = stats.reshape(grp_size, dp_size, -1)[:, :, : 4 * row_share]
    stats = stats.reshape(grp_size, dp_size, 4, row_share)
    maxima, totals = stats[:, :, 0], stats[:, :, 1]
    row_max = jnp.max(maxima, axis=1)
    lift = jnp.exp(maxima - row_max[:, None])
    row_total = jnp.sum(lift * totals, axis=1)
    log_total = jnp.log(row_total)
    gap = maxima[1] - row_max[1][None] - log_total[1][None]
    cross_term = jnp.sum(lift[0] * (stats[1, :, 2] + gap * stats[1, :, 3]), axis=0) / row_total[0]

    token_index = lax.axis_index("mp") * row_share + lax.iota(jnp.int32, row_share)
    slab_index = token_index // slab_length
    position = token_index - slab_index * slab_length
    matches = slab_index[:, None] == lax.iota(jnp.int32, lengths.shape[0])[None, :]
    valid_len = jnp.sum(jnp.where(matches, lengths[None, :], 0), axis=1)
    valid_mask = (position < valid_len).astype(jnp.float32)
    valid_total = jnp.sum(lengths).astype(jnp.float32)
    token_loss = -valid_mask * cross_term
    here = lax.axis_index("dp")
    own_lift = lax.dynamic_index_in_dim(lift, here, axis=1, keepdims=False)
    factor = own_lift / row_total * (valid_mask / valid_total)[None]
    own_factor = jnp.where(is_target, factor[0], factor[1])
    other_factor = jnp.where(is_target, jnp.zeros_like(factor[0]), factor[0])
    weighted = (raised * own_factor[:, None] - incoming * other_factor[:, None]).astype(jnp.bfloat16)
    (all_weighted,) = exchange(8, (weighted,), ((whole_axis("mp"), "gather", 0),))
    summed = jnp.einsum(
        "tv,td->vd", all_weighted, draft_rows, preferred_element_type=jnp.float32
    )
    sign_factor = jnp.where(is_target, -1.0, 1.0).astype(jnp.float32)
    grad_terms = (sign_factor * summed).astype(jnp.bfloat16)[None]
    return (grad_terms, token_loss)


def solution(mesh):
    in_specs = (
        P(None, "mp", ("grp", "dp")),
        P(None, ("grp", "dp"), "mp"),
        P("grp", "dp", "mp"),
        P("dp", "mp"),
        P("mp"),
        P("mp"),
        P(),
    )
    out_specs = (P("grp", "dp", "mp"), P("mp"))
    return jax.shard_map(
        per_device, mesh=mesh, in_specs=in_specs, out_specs=out_specs, check_vma=False
    )
```

time: 317 us -> 283 us (0.89)
  Pallas kernels: 0 us -> 218 us
  waiting for transfers between devices: 219 us -> 10.1 us
  blocking collectives: 26.4 us -> 0 us
  between operations: 15.3 us -> 1.59 us
  matrix products: 40.3 us -> 31.8 us
  other arithmetic: 11.8 us -> 15.6 us
    pallas_call x0 -> x8, Pallas kernels: none -> 218 us  [exchange(): pl.pallas_call(functools.partial(exchange_body, items), out_shape=shapes,...]
    psum x1 -> x0, waiting for transfers between devices: 104 us -> none  [per_device(): united = lax.psum(running, ('grp', 'dp'))]
    all_gather x3 -> x0, waiting for transfers between devices: 51.5 us -> none  [the longest x1 23.3 us: per_device(): segment = lax.all_gather(captured, 'mp', axis=1, tiled=True)]
    reduce_scatter x1 -> x0, waiting for transfers between devices: 42 us -> none  [per_device(): lax.psum_scatter(jnp.einsum('td,vd->tv', own_rows, head_rows, preferred_e...]
    psum x2 -> x0, blocking collectives: 14.7 us -> none  [the longest x1 8.41 us: per_device(): cross_term = lax.psum(jnp.sum(target_probs * draft_logs, axis=1), 'dp')]
    unnamed x1 -> x0, blocking collectives: 11.7 us -> none
    ppermute x1, waiting for transfers between devices: 20.3 us -> 10.1 us  [per_device(): lax.ppermute(raised.astype(jnp.bfloat16), 'grp', [(0, 1)])]
    dot_general x1, matrix products: 18.1 us -> 10.1 us  [per_device(): jnp.einsum('td,vd->tv', own_rows, head_rows, preferred_element_type=jnp.f...]
  transfers between devices with their start and end apart: 6 -> 1, of which waited for: 6 -> 1; matrix products, arithmetic and copies ran while one was open for 5% -> 0% of each run, Pallas kernels for 0% -> 0%
where the time goes in v1:
time: 283 us; the launch traced here: 281 us
  Pallas kernels  218 us (77%)
  matrix products  31.8 us (11%)
  other arithmetic  15.6 us (6%)
  waiting for transfers between devices  10.1 us (4%)
  starting transfers between devices  3.78 us (1%)
    pallas_call x8, Pallas kernels, exchange(): pl.pallas_call(functools.partial(exchange_body, items), out_shape=shapes,...  218 us
    dot_general x1, matrix products, per_device(): jnp.einsum('td,vd->tv', own_rows, head_rows, preferred_element_type=jnp.f...  10.1 us
    ppermute x1, waiting for transfers between devices, per_device(): lax.ppermute(raised.astype(jnp.bfloat16), 'grp', [(0, 1)])  10.1 us
    dot_general x1, matrix products, per_device(): jnp.einsum('tv,td->vd', all_weighted, draft_rows, preferred_element_type=...  9.98 us
    dot_general x2, matrix products, per_device(): jnp.dot(segment[layer_index], unite_weight[layer_index], preferred_elemen...  8.18 us
  transfers between devices with their start and end apart: 1, of which 1 were waited for; matrix products, arithmetic and copies ran while one was open for 0% of the time, Pallas kernels for 0%

profile of v1, /device:TPU:0, one launch (start us, length us, event | category | flops | bytes accessed | tf_op | source)
XLA Modules:
  0.0 281.4 jit_solution(14037236858155065540)
XLA Ops:
  0.6 26.2 %shard_map.86 = (bf16[3,256,1024]{2,1,0:T(8,128)(2,1)}, bf16[256,2048]{1,0:T(8,128)(2,1)}) custom-call(bf16[3,64,1024]{2,1,0:T(8,128)(2,1)} %refs_0_.1, bf16[64,2048]{1,0:T(8,128)(2,1)} %refs_1_.1), custom_call_target="tpu_custom_call" | custom-call | tf_op jit(solution)/shard_map/pallas_call | solution.py:93
  26.8 1.5 fusion.21
  28.3 0.0 copy-start.2
  28.4 3.7 %fusion.5 = f32[256,2048]{1,0:T(8,128)S(1)} fusion(bf16[3,1024,2048]{2,1,0:T(8,128)(2,1)} %param.8, bf16[3,256,1024]{2,1,0:T(8,128)(2,1)} %get-tuple-element.5), kind=kOutput, calls=%fused_computation.6 | convolution fusion | flops 1073741824 | bytes 6815744 | tf_op jit(solution)/shard_map/dot_general | solution.py:129
  32.1 0.0 copy-done.2
  32.1 3.5 %fusion.12 = f32[256,2048]{1,0:T(8,128)S(1)} fusion(f32[256,2048]{1,0:T(8,128)S(1)} %fusion.5, bf16[3,1024,2048]{2,1,0:T(8,128)(2,1)} %param.8, bf16[3,256,1024]{2,1,0:T(8,128)(2,1)S(1)} %copy-done.2), kind=kOutput, calls=%fused_computation.13 | convolution fusion | flops 1074266112 | bytes 8912896 | tf_op jit(solution)/shard_map/dot_general | solution.py:127
  35.6 4.5 %fusion.18.refs_0_ = bf16[256,2048]{1,0:T(8,128)(2,1)} fusion(f32[256,2048]{1,0:T(8,128)S(1)} %fusion.12, bf16[3,1024,2048]{2,1,0:T(8,128)(2,1)} %param.8, bf16[3,256,1024]{2,1,0:T(8,128)(2,1)S(1)} %copy-done.2), kind=kOutput, calls=%fused_computation.17 | convolution fusion | flops 1074790400 | bytes 7864320 | tf_op jit(solution)/shard_map/dot_general | solution.py:129
  40.1 0.0 copy-start.4
  40.1 27.7 %shard_map.87 = bf16[256,2048]{1,0:T(8,128)(2,1)} custom-call(bf16[256,2048]{1,0:T(8,128)(2,1)} %fusion.18.refs_0_), custom_call_target="tpu_custom_call" | custom-call | tf_op jit(solution)/shard_map/pallas_call | solution.py:93
  67.8 0.0 copy-start.1
  67.8 0.0 copy-start.3
  67.8 1.5 convert_reduce_fusion
  69.3 0.1 multiply_reduce_fusion
  69.4 0.7 fusion.38.refs_0_
  70.1 4.0 %shard_map.88 = f32[4,8,128]{2,1,0:T(8,128)} custom-call(f32[1,8,128]{2,1,0:T(8,128)} %fusion.38.refs_0_), custom_call_target="tpu_custom_call" | custom-call | tf_op jit(solution)/shard_map/pallas_call | solution.py:93
  74.1 0.7 reduce_sum.111
  74.8 0.1 add_rsqrt_fusion
  74.9 0.0 copy-done.4
  74.9 0.8 multiply_convert_fusion.1.refs_0_
  75.6 26.2 %shard_map.89 = bf16[256,2048]{1,0:T(8,128)(2,1)} custom-call(bf16[32,2048]{1,0:T(8,128)(2,1)} %multiply_convert_fusion.1.refs_0_), custom_call_target="tpu_custom_call" | custom-call | tf_op jit(solution)/shard_map/pallas_call | solution.py:93
  101.9 0.0 copy-done.1
  101.9 0.0 copy-done.3
  101.9 0.6 fusion.28
  102.5 10.1 %fusion.1.refs_0_ = f32[2,2,64,4000]{3,2,1,0:T(8,128)} fusion(bf16[2,2,64,2048]{3,2,1,0:T(8,128)(2,1)S(1)} %bitcast.85, bf16[1,4000,2048]{2,1,0:T(8,128)(2,1)} %param.9), kind=kOutput, calls=%fused_computation.2 | convolution fusion | flops 4194304000 | bytes 21528576 | tf_op jit(solution)/shard_map/td,vd->tv/dot_general | solution.py:151
  112.6 64.7 %shard_map.90 = f32[2,2,64,4000]{3,2,1,0:T(8,128)} custom-call(f32[2,2,64,4000]{3,2,1,0:T(8,128)} %fusion.1.refs_0_), custom_call_target="tpu_custom_call" | custom-call | tf_op jit(solution)/shard_map/pallas_call | solution.py:93
  177.2 3.8 %fusion.24.refs_0_ = f32[2,64,4000]{2,1,0:T(8,128)} fusion(f32[2,2,64,4000]{3,2,1,0:T(8,128)} %shard_map.90), kind=kLoop, calls=%fused_computation.22 | loop fusion | flops 512000 | bytes 6144000 | tf_op jit(solution)/shard_map/add | solution.py:157
  181.0 34.4 %shard_map.91 = f32[2,64,4000]{2,1,0:T(8,128)} custom-call(f32[2,64,4000]{2,1,0:T(8,128)} %fusion.24.refs_0_), custom_call_target="tpu_custom_call" | custom-call | tf_op jit(solution)/shard_map/pallas_call | solution.py:93
  215.5 1.8 reduce_sum.112
  217.3 0.0 copy-start.5
  217.3 0.2 reduce_max.18
  217.5 0.2 fusion.29
  217.7 3.8 %collective-permute-start = (bf16[64,4000]{1,0:T(8,128)(2,1)S(1)}, bf16[64,4000]{1,0:T(8,128)(2,1)S(1)}, u32[]{:S(2)}, u32[]{:S(2)}) collective-permute-start(bf16[64,4000]{1,0:T(8,128)(2,1)S(1)} %fusion.29), channel_id=1, source_target_pairs={{0,16},{1,17},{2,18},{3,19},{4,20},{5,21},{6,22},{7,23},{8,24},{9,... | collective-permute-start | bytes 1536008 | tf_op jit(solution)/shard_map/ppermute | solution.py:164
  221.5 0.0 copy-done.5
  221.5 0.6 reduce_sum.118
  222.8 0.1 select_reduce_fusion
  222.9 10.1 %collective-permute-done = bf16[64,4000]{1,0:T(8,128)(2,1)S(1)} collective-permute-done((bf16[64,4000]{1,0:T(8,128)(2,1)S(1)}, bf16[64,4000]{1,0:T(8,128)(2,1)S(1)}, u32[]{:S(2)}, u32[]{:S(2)}) %collective-permute-start) | collective-permute-done | bytes 512032 | tf_op jit(solution)/shard_map/ppermute | solution.py:164
  233.0 0.5 fusion.30
  233.5 0.7 fusion.37.refs_0_
  234.2 10.6 %shard_map.92 = f32[8,8,128]{2,1,0:T(8,128)} custom-call(f32[1,8,128]{2,1,0:T(8,128)} %fusion.37.refs_0_), custom_call_target="tpu_custom_call" | custom-call | tf_op jit(solution)/shard_map/pallas_call | solution.py:93
  244.8 0.8 reshape.100
  245.6 0.1 reshape.101
  245.9 0.5 fusion.43
  246.4 0.0 copy-start
  246.4 1.1 fusion.27.refs_0_
  247.5 23.9 %shard_map.93 = bf16[256,4000]{1,0:T(8,128)(2,1)} custom-call(bf16[64,4000]{1,0:T(8,128)(2,1)} %fusion.27.refs_0_), custom_call_target="tpu_custom_call" | custom-call | tf_op jit(solution)/shard_map/pallas_call | solution.py:93
  271.4 0.0 copy-done
  271.4 10.0 %fusion = bf16[1,4000,2048]{2,1,0:T(8,128)(2,1)} fusion(f32[]{:T(128)S(6)} %select_n.59, bf16[256,4000]{1,0:T(8,128)(2,1)} %shard_map.93, bf16[256,2048]{1,0:T(8,128)(2,1)S(1)} %copy-done), kind=kOutput, calls=%fused_computation.1 | convolution fusion | flops 4210688000 | bytes 19480580 | tf_op jit(solution)/shard_map/tv,td->vd/dot_general | solution.py:197
  (13 shorter events, 0.2 us)
Async XLA Ops:
  28.3 3.7 %copy-start.2 = (bf16[3,256,1024]{2,1,0:T(8,128)(2,1)S(1)}, bf16[3,256,1024]{2,1,0:T(8,128)(2,1)}, u32[]{:S(2)}) copy-start(bf16[3,256,1024]{2,1,0:T(8,128)(2,1)} %get-tuple-element.5) | copy-start | bytes 4718596
  40.1 34.8 %copy-start.4 = (f32[2048]{0:T(1024)S(1)}, f32[2048]{0:T(1024)}, u32[]{:S(2)}) copy-start(f32[2048]{0:T(1024)} %param.12) | copy-start | bytes 24580
  67.8 34.1 %copy-start.1 = (bf16[256,2048]{1,0:T(8,128)(2,1)S(1)}, bf16[256,2048]{1,0:T(8,128)(2,1)}, u32[]{:S(2)}) copy-start(bf16[256,2048]{1,0:T(8,128)(2,1)} %get-tuple-element.4) | copy-start | bytes 3145732
  67.8 34.1 %copy-start.3 = (f32[2048]{0:T(1024)S(1)}, f32[2048]{0:T(1024)}, u32[]{:S(2)}) copy-start(f32[2048]{0:T(1024)} %param.11) | copy-start | bytes 24580
  217.3 4.2 %copy-start.5 = (s32[4]{0:T(128)S(1)}, s32[4]{0:T(128)}, u32[]{:S(2)}) copy-start(s32[4]{0:T(128)} %param.13) | copy-start | bytes 52
  217.7 15.3 %collective-permute-start = (bf16[64,4000]{1,0:T(8,128)(2,1)S(1)}, bf16[64,4000]{1,0:T(8,128)(2,1)S(1)}, u32[]{:S(2)}, u32[]{:S(2)}) collective-permute-start(bf16[64,4000]{1,0:T(8,128)(2,1)S(1)} %fusion.29), channel_id=1, source_target_pairs={{0,16},{1,17},{2,18},{3,19},{4,20},{5,21},{6,22},{7,23},{8,24},{9,... | collective-permute-start | bytes 1536008 | tf_op jit(solution)/shard_map/ppermute | solution.py:164
  246.4 25.0 %copy-start = (bf16[256,2048]{1,0:T(8,128)(2,1)S(1)}, bf16[256,2048]{1,0:T(8,128)(2,1)}, u32[]{:S(2)}) copy-start(bf16[256,2048]{1,0:T(8,128)(2,1)} %shard_map.89) | copy-start | bytes 3145732

commit v2 on v1

--- a/solution.py
+++ b/solution.py
@@ -33,9 +33,9 @@
     return (count, lax.div(index, 2), lambda p: {"mp": p * 2 + lax.rem(index, 2)})
 
 
-def rows_at(ref, dim, index, size):
-    window = pl.ds(pl.multiple_of(index * size, size), size)
-    return ref.at[(slice(None),) * dim + (window,)]
+def window(ref, dim, index, size):
+    start = index * size if isinstance(index, int) else pl.multiple_of(index * size, size)
+    return ref.at[(slice(None),) * dim + (pl.ds(start, size),)]
 
 
 def exchange_body(items, *refs):
@@ -54,28 +54,34 @@
     pl.semaphore_wait(barrier, total)
     copies = []
     slot = 0
-    for number, ((_, kind, dim), (n, me, place)) in enumerate(zip(items, groups)):
+    for number, ((_, kind, dim, cut, pieces), (n, me, place)) in enumerate(zip(items, groups)):
         source, target = ins[number], outs[number]
-        size = target.shape[dim] // n
-        landing = rows_at(target, dim, me, size)
+        step = source.shape[cut] // pieces
         for k in range(1, n):
             peer = lax.rem(me + k, n)
-            sent = source if kind == "gather" else rows_at(source, dim, peer, size)
-            copy = pltpu.make_async_remote_copy(
-                src_ref=sent,
-                dst_ref=landing,
-                send_sem=send_sem.at[slot],
-                recv_sem=recv_sem.at[slot],
-                device_id=place(peer),
-                device_id_type=MESH,
+            if kind == "gather":
+                sent, landing = source, window(target, dim, me, source.shape[dim])
+            else:
+                size = source.shape[dim] // n
+                sent, landing = window(source, dim, peer, size), window(target, dim, k - 1, size)
+            for piece in range(pieces):
+                copy = pltpu.make_async_remote_copy(
+                    src_ref=sent if pieces == 1 else window(sent, cut, piece, step),
+                    dst_ref=landing if pieces == 1 else window(landing, cut, piece, step),
+                    send_sem=send_sem.at[slot],
+                    recv_sem=recv_sem.at[slot],
+                    device_id=place(peer),
+                    device_id_type=MESH,
+                )
+                copy.start()
+                copies.append(copy)
+                slot += 1
+        if kind == "gather":
+            own = pltpu.make_async_copy(
+                source, window(target, dim, me, source.shape[dim]), local_sem.at[number]
             )
-            copy.start()
-            copies.append(copy)
-            slot += 1
-        kept = source if kind == "gather" else rows_at(source, dim, me, size)
-        own = pltpu.make_async_copy(kept, landing, local_sem.at[number])
-        own.start()
-        copies.append(own)
+            own.start()
+            copies.append(own)
     for copy in copies:
         copy.wait()
 
@@ -83,12 +89,11 @@
 def exchange(number, arrays, items):
     shapes = []
     slots = 0
-    for array, (group, kind, dim) in zip(arrays, items):
+    for array, (group, kind, dim, cut, pieces) in zip(arrays, items):
         n = group()[0]
-        slots += n - 1
+        slots += (n - 1) * pieces
         shape = list(array.shape)
-        if kind == "gather":
-            shape[dim] *= n
+        shape[dim] = shape[dim] * n if kind == "gather" else shape[dim] // n * (n - 1)
         shapes.append(jax.ShapeDtypeStruct(tuple(shape), array.dtype))
     return pl.pallas_call(
         functools.partial(exchange_body, items),
@@ -104,6 +109,15 @@
     )(*arrays)
 
 
+def summed_over(number, parts, group, pieces):
+    (arrived,) = exchange(number, (parts,), ((group, "swap", 0, 1, pieces),))
+    own = lax.dynamic_index_in_dim(parts, group()[1], axis=0, keepdims=False)
+    total = own.astype(jnp.float32)
+    for k in range(arrived.shape[0]):
+        total = total + arrived[k].astype(jnp.float32)
+    return total
+
+
 def as_tile(parts):
     flat = jnp.concatenate([part.reshape(-1) for part in parts])
     padded = -(-flat.shape[0] // 1024) * 1024
@@ -118,11 +132,9 @@
     slab_length = final_hidden.shape[0]
     is_target = lax.axis_index("grp") == 0
     head_rows = heads[0]
-    segment, last = exchange(
-        1,
-        (captured, final_hidden),
-        ((whole_axis("mp"), "gather", 1), (whole_axis("dp"), "gather", 0)),
-    )
+    last = lax.all_gather(final_hidden, "dp", axis=0, tiled=True)
+    layers = captured.shape[0]
+    (segment,) = exchange(1, (captured,), ((whole_axis("mp"), "gather", 1, 0, layers),))
     tokens = last.shape[0]
     running = jnp.dot(segment[0], unite_weight[0], preferred_element_type=jnp.float32)
     for layer_index in range(1, segment.shape[0]):
@@ -130,33 +142,33 @@
             segment[layer_index], unite_weight[layer_index], preferred_element_type=jnp.float32
         )
     members = grp_size * dp_size
-    (arrived,) = exchange(2, (running.astype(PARTIAL),), ((both_axes, "swap", 0),))
     share = tokens // members
-    arrived = arrived.reshape(members, share, -1)
-    united = jnp.sum(arrived.astype(jnp.float32), axis=0)
+    united = summed_over(2, running.astype(PARTIAL).reshape(members, share, -1), both_axes, 1)
     last_values = last.astype(jnp.float32)
     (squares,) = exchange(
         3,
         (as_tile([jnp.sum(united * united, axis=1), jnp.sum(last_values * last_values, axis=1)]),),
-        ((whole_axis("mp"), "gather", 0),),
+        ((whole_axis("mp"), "gather", 0, 1, 1),),
     )
     squares = jnp.sum(squares, axis=0).reshape(-1)
     draft_scale = lax.rsqrt(squares[:share] / model_width + EPSILON)
     target_scale = lax.rsqrt(squares[share : share + tokens] / model_width + EPSILON)
     draft_part = (united * draft_scale[:, None] * draft_gain[None, :]).astype(jnp.bfloat16)
     target_rows = (last_values * target_scale[:, None] * target_gain[None, :]).astype(jnp.bfloat16)
-    (draft_rows,) = exchange(4, (draft_part,), ((both_axes, "gather", 0),))
+    (draft_rows,) = exchange(4, (draft_part,), ((both_axes, "gather", 0, 1, 1),))
     own_rows = jnp.where(is_target, target_rows, draft_rows)
     row_share = tokens // mp_size
     partial_logits = jnp.einsum(
         "td,vd->tv", own_rows, head_rows, preferred_element_type=jnp.float32
     )
     vocab = partial_logits.shape[1]
-    by_core = partial_logits.reshape(mp_size // 2, 2, row_share, vocab)
-    (by_core,) = exchange(5, (by_core,), ((pair, "swap", 1),))
-    by_chip = by_core[:, 0] + by_core[:, 1]
-    (by_chip,) = exchange(6, (by_chip,), ((across, "swap", 0),))
-    logits = jnp.sum(by_chip, axis=0)
+    width = -(-vocab // 128) * 128
+    partial_logits = jnp.pad(partial_logits, ((0, 0), (0, width - vocab)))
+    by_core = partial_logits.reshape(mp_size // 2, 2, row_share, width)
+    pieces = row_share // 8
+    (swapped,) = exchange(5, (by_core,), ((pair, "swap", 1, 2, pieces),))
+    by_chip = swapped[:, 0] + lax.dynamic_index_in_dim(by_core, pair()[1], axis=1, keepdims=False)
+    logits = summed_over(6, by_chip, across, pieces)[:, :vocab]
     local_max = jnp.max(logits, axis=1)
     shifted = logits - local_max[:, None]
     raised = jnp.exp(shifted)
@@ -167,7 +179,7 @@
     (stats,) = exchange(
         7,
         (as_tile([local_max, local_total, crossed, incoming_total]),),
-        ((both_axes, "gather", 0),),
+        ((both_axes, "gather", 0, 1, 1),),
     )
     stats = stats.reshape(grp_size, dp_size, -1)[:, :, : 4 * row_share]
     stats = stats.reshape(grp_size, dp_size, 4, row_share)
@@ -193,7 +205,7 @@
     own_factor = jnp.where(is_target, factor[0], factor[1])
     other_factor = jnp.where(is_target, jnp.zeros_like(factor[0]), factor[0])
     weighted = (raised * own_factor[:, None] - incoming * other_factor[:, None]).astype(jnp.bfloat16)
-    (all_weighted,) = exchange(8, (weighted,), ((whole_axis("mp"), "gather", 0),))
+    all_weighted = lax.all_gather(weighted, "mp", axis=0, tiled=True)
     summed = jnp.einsum(
         "tv,td->vd", all_weighted, draft_rows, preferred_element_type=jnp.float32
     )

time: 283 us -> 225 us (0.80)
  Pallas kernels: 218 us -> 120 us
  waiting for transfers between devices: 10.1 us -> 31.8 us
  between operations: 1.59 us -> 15 us
  local copies, waits for them, and re-layouts: 0.92 us -> 5.49 us
    pallas_call x8 -> x7, Pallas kernels: 218 us -> 120 us  [exchange(): pl.pallas_call(functools.partial(exchange_body, items), out_shape=shapes,...]
    all_gather x0 -> x2, waiting for transfers between devices: none -> 22.1 us  [the longest x1 22.1 us: per_device(): all_weighted = lax.all_gather(weighted, 'mp', axis=0, tiled=True)]
    unnamed x0 -> x1, matrix products: none -> 12.3 us
    dot_general x1 -> x0, matrix products: 10.1 us -> none  [per_device(): jnp.einsum('td,vd->tv', own_rows, head_rows, preferred_element_type=jnp.f...]
    pad x0 -> x1, local copies, waits for them, and re-layouts: none -> 4.57 us  [per_device(): partial_logits = jnp.pad(partial_logits, ((0, 0), (0, width - vocab)))]
    reduce_sum x2 -> x0, other arithmetic: 3.31 us -> none  [the longest x1 1.84 us: per_device(): logits = jnp.sum(by_chip, axis=0)]
  transfers between devices with their start and end apart: 1 -> 3, of which waited for: 1 -> 2; matrix products, arithmetic and copies ran while one was open for 0% -> 7% of each run, Pallas kernels for 0% -> 21%
where the time goes in v2:
time: 225 us; the launch traced here: 224 us
  Pallas kernels  120 us (53%)
  matrix products  34 us (15%)
  waiting for transfers between devices  31.8 us (14%)
  between operations  15 us (7%)
  other arithmetic  14.6 us (6%)
  local copies, waits for them, and re-layouts  5.49 us (2%)
  starting transfers between devices  3.32 us (1%)
    pallas_call x7, Pallas kernels, exchange(): pl.pallas_call(functools.partial(exchange_body, items), out_shape=shapes,...  120 us
    all_gather x1, waiting for transfers between devices, per_device(): all_weighted = lax.all_gather(weighted, 'mp', axis=0, tiled=True)  22.1 us
    unnamed x1, matrix products  12.3 us
    dot_general x1, matrix products, per_device(): jnp.einsum('tv,td->vd', all_weighted, draft_rows, preferred_element_type=...  9.95 us
    ppermute x1, waiting for transfers between devices, per_device(): lax.ppermute(raised.astype(jnp.bfloat16), 'grp', [(0, 1)])  8.96 us
    dot_general x2, matrix products, per_device(): jnp.dot(segment[layer_index], unite_weight[layer_index], preferred_elemen...  8.22 us
    pad x1, local copies, waits for them, and re-layouts, per_device(): partial_logits = jnp.pad(partial_logits, ((0, 0), (0, width - vocab)))  4.57 us
  transfers between devices with their start and end apart: 3, of which 2 were waited for; matrix products, arithmetic and copies ran while one was open for 7% of the time, Pallas kernels for 21%

profile of v2, /device:TPU:0, one launch (start us, length us, event | category | flops | bytes accessed | tf_op | source)
XLA Modules:
  0.0 224.1 jit_solution(1708537289236702843)
XLA Ops:
  7.2 0.0 all-gather.3.cloned.1.call-start
  7.2 0.7 all-gather.3.cloned.1.call-update
  7.9 0.0 all-gather.5.cloned.1.call-start
  8.0 20.9 %shard_map.86 = bf16[3,256,1024]{2,1,0:T(8,128)(2,1)} custom-call(bf16[3,64,1024]{2,1,0:T(8,128)(2,1)} %refs_0_.1), custom_call_target="tpu_custom_call" | custom-call | tf_op jit(solution)/shard_map/pallas_call | solution.py:98
  28.9 0.0 copy-start.1
  28.9 3.7 %fusion.5 = f32[256,2048]{1,0:T(8,128)S(1)} fusion(bf16[3,1024,2048]{2,1,0:T(8,128)(2,1)} %param.8, bf16[3,256,1024]{2,1,0:T(8,128)(2,1)} %shard_map.86), kind=kOutput, calls=%fused_computation.6 | convolution fusion | flops 1073741824 | bytes 6815744 | tf_op jit(solution)/shard_map/dot_general | solution.py:141
  32.6 0.0 copy-done.1
  32.6 3.5 %fusion.12 = f32[256,2048]{1,0:T(8,128)S(1)} fusion(f32[256,2048]{1,0:T(8,128)S(1)} %fusion.5, bf16[3,1024,2048]{2,1,0:T(8,128)(2,1)} %param.8, bf16[3,256,1024]{2,1,0:T(8,128)(2,1)S(1)} %copy-done.1), kind=kOutput, calls=%fused_computation.13 | convolution fusion | flops 1074266112 | bytes 8912896 | tf_op jit(solution)/shard_map/dot_general | solution.py:139
  36.2 4.5 %fusion.18 = bf16[256,2048]{1,0:T(8,128)(2,1)} fusion(f32[256,2048]{1,0:T(8,128)S(1)} %fusion.12, bf16[3,1024,2048]{2,1,0:T(8,128)(2,1)} %param.8, bf16[3,256,1024]{2,1,0:T(8,128)(2,1)S(1)} %copy-done.1), kind=kOutput, calls=%fused_computation.17 | convolution fusion | flops 1074790400 | bytes 7864320 | tf_op jit(solution)/shard_map/dot_general | solution.py:141
  40.7 0.0 copy-start.4
  40.7 26.9 %shard_map.87 = bf16[7,32,2048]{2,1,0:T(8,128)(2,1)} custom-call(bf16[8,32,2048]{2,1,0:T(8,128)(2,1)} %bitcast.93), custom_call_target="tpu_custom_call" | custom-call | tf_op jit(solution)/shard_map/pallas_call | solution.py:98
  67.5 0.0 copy-start.5
  67.6 1.5 fusion.42
  69.1 0.0 all-gather.3.cloned.1.call-done
  69.1 0.0 copy-start.3
  69.1 1.6 fusion.21
  70.7 0.7 fusion.46.refs_0_
  71.4 4.0 %shard_map.88 = f32[4,8,128]{2,1,0:T(8,128)} custom-call(f32[1,8,128]{2,1,0:T(8,128)} %fusion.46.refs_0_), custom_call_target="tpu_custom_call" | custom-call | tf_op jit(solution)/shard_map/pallas_call | solution.py:98
  75.4 0.7 reduce_sum.92
  76.1 0.1 add_rsqrt_fusion
  76.2 0.0 copy-done.4
  76.2 0.8 fusion.44.refs_0_
  77.0 27.4 %shard_map.89 = bf16[256,2048]{1,0:T(8,128)(2,1)} custom-call(bf16[32,2048]{1,0:T(8,128)(2,1)} %fusion.44.refs_0_), custom_call_target="tpu_custom_call" | custom-call | tf_op jit(solution)/shard_map/pallas_call | solution.py:98
  104.4 0.0 copy-done.5
  104.4 0.0 copy-done.3
  104.4 12.3 %fusion.1 = f32[256,4000]{1,0:T(8,128)} fusion(bf16[1,4000,2048]{2,1,0:T(8,128)(2,1)} %param.9, bf16[256,2048]{1,0:T(8,128)(2,1)} %shard_map.89, bf16[256,2048]{1,0:T(8,128)(2,1)S(1)} %copy-done.3, f32[2048]{0:T(1024)S(1)} %copy-done.5, f32[256]{0:T(256)S(1)} %add_rsqrt_fusion, pred[]{:T(512)S(6)} %eq.16), kind=kOutput, calls=%fused_computation.2 | convolution fusion | flops 4196925440 | bytes 22586368
  116.7 4.6 %pad.13.clone = f32[256,4096]{1,0:T(8,128)} pad(f32[256,4000]{1,0:T(8,128)} %fusion.1, f32[]{:T(128)} %constant.68.clone.1), padding=0_0x0_96 | pad | bytes 8290308 | tf_op jit(solution)/shard_map/jit(_pad)/pad | solution.py:166
  121.3 4.7 %shard_map.90 = f32[2,1,64,4096]{3,2,1,0:T(8,128)} custom-call(f32[2,2,64,4096]{3,2,1,0:T(8,128)} %bitcast.90), custom_call_target="tpu_custom_call" | custom-call | tf_op jit(solution)/shard_map/pallas_call | solution.py:98
  125.9 3.8 %bitcast_add_fusion = f32[2,1,64,4096]{3,2,0,1:T(8,128)} fusion(f32[2,1,64,4096]{3,2,1,0:T(8,128)} %shard_map.90, f32[2,2,64,4096]{3,2,1,0:T(8,128)} %bitcast.91, s32[]{:T(128)S(6)} %select_n.75), kind=kLoop, calls=%fused_computation.21 | loop fusion | flops 524288 | bytes 6291460 | tf_op jit(solution)/shard_map/add | solution.py:170
  129.7 0.0 copy-start
  129.7 25.7 %shard_map.91 = f32[1,64,4096]{2,1,0:T(8,128)} custom-call(f32[2,64,4096]{2,1,0:T(8,128)} %bitcast.92), custom_call_target="tpu_custom_call" | custom-call | tf_op jit(solution)/shard_map/pallas_call | solution.py:98
  155.4 0.0 copy-done
  155.4 1.3 fusion.29
  156.8 0.0 copy-start.6
  156.8 0.1 slice_reduce_fusion
  156.9 0.2 fusion.34
  157.2 3.2 %collective-permute-start = (bf16[64,4000]{1,0:T(8,128)(2,1)S(1)}, bf16[64,4000]{1,0:T(8,128)(2,1)S(1)}, u32[]{:S(2)}, u32[]{:S(2)}) collective-permute-start(bf16[64,4000]{1,0:T(8,128)(2,1)S(1)} %fusion.34), channel_id=1, source_target_pairs={{0,16},{1,17},{2,18},{3,19},{4,20},{5,21},{6,22},{7,23},{8,24},{9,... | collective-permute-start | bytes 1536008 | tf_op jit(solution)/shard_map/ppermute | solution.py:176
  160.4 0.0 copy-done.6
  160.4 0.6 reduce_sum.98
  161.8 0.1 select_reduce_fusion
  161.9 0.0 copy-start.2
  161.9 9.0 %collective-permute-done = bf16[64,4000]{1,0:T(8,128)(2,1)S(1)} collective-permute-done((bf16[64,4000]{1,0:T(8,128)(2,1)S(1)}, bf16[64,4000]{1,0:T(8,128)(2,1)S(1)}, u32[]{:S(2)}, u32[]{:S(2)}) %collective-permute-start) | collective-permute-done | bytes 512032 | tf_op jit(solution)/shard_map/ppermute | solution.py:176
  170.8 0.5 fusion.35
  171.4 0.7 fusion.45.refs_0_
  172.0 10.5 %shard_map.92 = f32[8,8,128]{2,1,0:T(8,128)} custom-call(f32[1,8,128]{2,1,0:T(8,128)} %fusion.45.refs_0_), custom_call_target="tpu_custom_call" | custom-call | tf_op jit(solution)/shard_map/pallas_call | solution.py:98
  182.5 0.8 reshape.120
  183.3 0.1 reshape.121
  183.5 1.1 fusion.26
  184.6 0.0 all-gather.5.cloned.1.call-update
  184.7 0.5 fusion.51
  185.2 22.1 %all-gather.5.cloned.1.call-done = bf16[256,4000]{1,0:T(8,128)(2,1)} async-done(((bf16[64,4000]{1,0:T(8,128)(2,1)}), bf16[256,4000]{1,0:T(8,128)(2,1)}) %all-gather.5.cloned.1.call-update) | async-done | bytes 2048016 | tf_op jit(solution)/shard_map/all_gather | solution.py:208
  207.3 0.0 copy-done.2
  207.3 10.0 %fusion = bf16[1,4000,2048]{2,1,0:T(8,128)(2,1)} fusion(f32[]{:T(128)S(6)} %select_n.71, bf16[256,4000]{1,0:T(8,128)(2,1)} %all-gather.5.cloned.1.call-done, bf16[256,2048]{1,0:T(8,128)(2,1)S(1)} %copy-done.2), kind=kOutput, calls=%fused_computation.1 | convolution fusion | flops 4210688000 | bytes 19480580 | tf_op jit(solution)/shard_map/tv,td->vd/dot_general | solution.py:209
  (13 shorter events, 0.2 us)
Async XLA Ops:
  7.2 62.0 %all-gather.3.cloned.1.call-start = ((), (), s32[]{:S(2)}) async-start(), calls=%async_computation | async-start | bytes 1310720 | tf_op jit(solution)/shard_map/all_gather | solution.py:135
  7.9 199.4 %all-gather.5.cloned.1.call-start = ((), (), s32[]{:S(2)}) async-start(), calls=%async_computation.1 | async-start | bytes 2621440 | tf_op jit(solution)/shard_map/all_gather | solution.py:208
  28.9 3.8 %copy-start.1 = (bf16[3,256,1024]{2,1,0:T(8,128)(2,1)S(1)}, bf16[3,256,1024]{2,1,0:T(8,128)(2,1)}, u32[]{:S(2)}) copy-start(bf16[3,256,1024]{2,1,0:T(8,128)(2,1)} %shard_map.86) | copy-start | bytes 4718596
  40.7 35.6 %copy-start.4 = (f32[2048]{0:T(1024)S(1)}, f32[2048]{0:T(1024)}, u32[]{:S(2)}) copy-start(f32[2048]{0:T(1024)} %param.12) | copy-start | bytes 24580
  67.5 36.8 %copy-start.5 = (f32[2048]{0:T(1024)S(1)}, f32[2048]{0:T(1024)}, u32[]{:S(2)}) copy-start(f32[2048]{0:T(1024)} %param.11) | copy-start | bytes 24580
  69.1 35.2 %copy-start.3 = (bf16[256,2048]{1,0:T(8,128)(2,1)S(1)}, bf16[256,2048]{1,0:T(8,128)(2,1)}, u32[]{:S(2)}) copy-start(bf16[256,2048]{1,0:T(8,128)(2,1)} %all-gather.3.cloned.1.call-done) | copy-start | bytes 3145732
  129.7 25.7 %copy-start = (f32[2,1,64,4096]{3,2,0,1:T(8,128)S(1)}, f32[2,1,64,4096]{3,2,0,1:T(8,128)}, u32[]{:S(2)}) copy-start(f32[2,1,64,4096]{3,2,0,1:T(8,128)} %bitcast_add_fusion) | copy-start | bytes 6291460
  156.8 3.6 %copy-start.6 = (s32[4]{0:T(128)S(1)}, s32[4]{0:T(128)}, u32[]{:S(2)}) copy-start(s32[4]{0:T(128)} %param.13) | copy-start | bytes 52
  157.2 13.7 %collective-permute-start = (bf16[64,4000]{1,0:T(8,128)(2,1)S(1)}, bf16[64,4000]{1,0:T(8,128)(2,1)S(1)}, u32[]{:S(2)}, u32[]{:S(2)}) collective-permute-start(bf16[64,4000]{1,0:T(8,128)(2,1)S(1)} %fusion.34), channel_id=1, source_target_pairs={{0,16},{1,17},{2,18},{3,19},{4,20},{5,21},{6,22},{7,23},{8,24},{9,... | collective-permute-start | bytes 1536008 | tf_op jit(solution)/shard_map/ppermute | solution.py:176
  161.9 45.5 %copy-start.2 = (bf16[256,2048]{1,0:T(8,128)(2,1)S(1)}, bf16[256,2048]{1,0:T(8,128)(2,1)}, u32[]{:S(2)}) copy-start(bf16[256,2048]{1,0:T(8,128)(2,1)} %shard_map.89) | copy-start | bytes 3145732
Sparse Core Ops, SparseCore 0:
  9.6 30.6 all-gather.2
  184.8 22.5 all-gather.4

commit v3 on v2

--- a/solution.py
+++ b/solution.py
@@ -118,6 +118,67 @@
     return total
 
 
+def gathered_in_chip(numbers, array, cut, pieces):
+    lifted = array[:, None, None]
+    (lifted,) = exchange(numbers[0], (lifted,), ((across, "gather", 1, cut, pieces),))
+    (lifted,) = exchange(numbers[1], (lifted,), ((pair, "gather", 2, cut, pieces),))
+    return lifted.reshape(array.shape[0], -1, array.shape[2])
+
+
+def unite_body(captured_ref, weight_ref, out_ref, total):
+    layer = pl.program_id(1)
+
+    @pl.when(layer == 0)
+    def _():
+        total[...] = jnp.zeros_like(total)
+
+    total[...] += jnp.dot(captured_ref[0], weight_ref[0], preferred_element_type=jnp.float32)
+
+    @pl.when(layer == pl.num_programs(1) - 1)
+    def _():
+        out_ref[...] = total[...].astype(out_ref.dtype)
+
+
+def unite(segment, weight, tile=512):
+    layers, tokens, depth = segment.shape
+    columns = weight.shape[2]
+    tile = min(tile, columns)
+    return pl.pallas_call(
+        unite_body,
+        out_shape=jax.ShapeDtypeStruct((tokens, columns), PARTIAL),
+        grid=(columns // tile, layers),
+        in_specs=[
+            pl.BlockSpec((1, tokens, depth), lambda c, l: (l, 0, 0)),
+            pl.BlockSpec((1, depth, tile), lambda c, l: (l, 0, c)),
+        ],
+        out_specs=pl.BlockSpec((tokens, tile), lambda c, l: (0, c)),
+        scratch_shapes=[pltpu.VMEM((tokens, tile), jnp.float32)],
+        compiler_params=pltpu.CompilerParams(vmem_limit_bytes=32 * 2**20),
+    )(segment, weight)
+
+
+def logits_body(rows_ref, head_ref, out_ref):
+    out_ref[...] = lax.dot_general(
+        rows_ref[...], head_ref[0], (((1,), (1,)), ((), ())), preferred_element_type=jnp.float32
+    )
+
+
+def logits_of(rows, head, width, tile=512):
+    tokens, depth = rows.shape
+    tile = min(tile, width)
+    return pl.pallas_call(
+        logits_body,
+        out_shape=jax.ShapeDtypeStruct((tokens, width), jnp.float32),
+        grid=(pl.cdiv(width, tile),),
+        in_specs=[
+            pl.BlockSpec((tokens, depth), lambda v: (0, 0)),
+            pl.BlockSpec((1, tile, depth), lambda v: (0, v, 0)),
+        ],
+        out_specs=pl.BlockSpec((tokens, tile), lambda v: (0, v)),
+        compiler_params=pltpu.CompilerParams(vmem_limit_bytes=32 * 2**20),
+    )(rows, head)
+
+
 def as_tile(parts):
     flat = jnp.concatenate([part.reshape(-1) for part in parts])
     padded = -(-flat.shape[0] // 1024) * 1024
@@ -131,19 +192,13 @@
     model_width = final_hidden.shape[1] * mp_size
     slab_length = final_hidden.shape[0]
     is_target = lax.axis_index("grp") == 0
-    head_rows = heads[0]
     last = lax.all_gather(final_hidden, "dp", axis=0, tiled=True)
-    layers = captured.shape[0]
-    (segment,) = exchange(1, (captured,), ((whole_axis("mp"), "gather", 1, 0, layers),))
+    segment = gathered_in_chip((1, 9), captured, 0, captured.shape[0])
     tokens = last.shape[0]
-    running = jnp.dot(segment[0], unite_weight[0], preferred_element_type=jnp.float32)
-    for layer_index in range(1, segment.shape[0]):
-        running = running + jnp.dot(
-            segment[layer_index], unite_weight[layer_index], preferred_element_type=jnp.float32
-        )
+    running = unite(segment, unite_weight)
     members = grp_size * dp_size
     share = tokens // members
-    united = summed_over(2, running.astype(PARTIAL).reshape(members, share, -1), both_axes, 1)
+    united = summed_over(2, running.reshape(members, share, -1), both_axes, 1)
     last_values = last.astype(jnp.float32)
     (squares,) = exchange(
         3,
@@ -158,17 +213,15 @@
     (draft_rows,) = exchange(4, (draft_part,), ((both_axes, "gather", 0, 1, 1),))
     own_rows = jnp.where(is_target, target_rows, draft_rows)
     row_share = tokens // mp_size
-    partial_logits = jnp.einsum(
-        "td,vd->tv", own_rows, head_rows, preferred_element_type=jnp.float32
-    )
-    vocab = partial_logits.shape[1]
+    vocab = heads.shape[1]
     width = -(-vocab // 128) * 128
-    partial_logits = jnp.pad(partial_logits, ((0, 0), (0, width - vocab)))
+    partial_logits = logits_of(own_rows, heads, width)
     by_core = partial_logits.reshape(mp_size // 2, 2, row_share, width)
     pieces = row_share // 8
     (swapped,) = exchange(5, (by_core,), ((pair, "swap", 1, 2, pieces),))
     by_chip = swapped[:, 0] + lax.dynamic_index_in_dim(by_core, pair()[1], axis=1, keepdims=False)
-    logits = summed_over(6, by_chip, across, pieces)[:, :vocab]
+    logits = summed_over(6, by_chip, across, pieces)
+    logits = jnp.where(lax.broadcasted_iota(jnp.int32, logits.shape, 1) < vocab, logits, -1e30)
     local_max = jnp.max(logits, axis=1)
     shifted = logits - local_max[:, None]
     raised = jnp.exp(shifted)
@@ -205,7 +258,7 @@
     own_factor = jnp.where(is_target, factor[0], factor[1])
     other_factor = jnp.where(is_target, jnp.zeros_like(factor[0]), factor[0])
     weighted = (raised * own_factor[:, None] - incoming * other_factor[:, None]).astype(jnp.bfloat16)
-    all_weighted = lax.all_gather(weighted, "mp", axis=0, tiled=True)
+    all_weighted = gathered_in_chip((8, 10), weighted[None], 3, width // 1024 or 1)[0, :, :vocab]
     summed = jnp.einsum(
         "tv,td->vd", all_weighted, draft_rows, preferred_element_type=jnp.float32
     )

time: 225 us -> 273 us (1.21)
  Pallas kernels: 120 us -> 203 us
  matrix products: 34 us -> 9.98 us
  waiting for transfers between devices: 31.8 us -> 9.84 us
  local copies, waits for them, and re-layouts: 5.49 us -> 15.5 us
    pallas_call x7 -> x10, Pallas kernels: 120 us -> 190 us  [exchange(): pl.pallas_call(functools.partial(exchange_body, items), out_shape=shapes,...]
    all_gather x1 -> x0, waiting for transfers between devices: 22.1 us -> none  [per_device(): all_weighted = lax.all_gather(weighted, 'mp', axis=0, tiled=True)]
    unnamed x14 -> x22, local copies, waits for them, and re-layouts: 0.03 us -> 14.6 us
    pallas_call x0 -> x2, Pallas kernels: none -> 13 us  [the longest x1 6.75 us: unite(): pl.pallas_call(unite_body, out_shape=jax.ShapeDtypeStruct((tokens, column...]
    unnamed x1 -> x0, matrix products: 12.3 us -> none
    dot_general x3 -> x0, matrix products: 11.8 us -> none  [the longest x2 8.22 us: per_device(): jnp.dot(segment[layer_index], unite_weight[layer_index], preferred_elemen...]
    pad x1 -> x0, local copies, waits for them, and re-layouts: 4.57 us -> none  [per_device(): partial_logits = jnp.pad(partial_logits, ((0, 0), (0, width - vocab)))]
  transfers between devices with their start and end apart: 3 -> 2, of which waited for: 2 -> 1; matrix products, arithmetic and copies ran while one was open for 7% -> 1% of each run, Pallas kernels for 21% -> 27%
where the time goes in v3:
time: 273 us
  Pallas kernels  203 us (74%)
  local copies, waits for them, and re-layouts  15.5 us (6%)
  other arithmetic  15.2 us (6%)
  between operations  15.1 us (6%)
  matrix products  9.98 us (4%)
  waiting for transfers between devices  9.84 us (4%)
  starting transfers between devices  3.88 us (1%)
    pallas_call x10, Pallas kernels, exchange(): pl.pallas_call(functools.partial(exchange_body, items), out_shape=shapes,...  190 us
    unnamed x22, local copies, waits for them, and re-layouts  14.6 us
    dot_general x1, matrix products, per_device(): jnp.einsum('tv,td->vd', all_weighted, draft_rows, preferred_element_type=...  9.98 us
    ppermute x1, waiting for transfers between devices, per_device(): lax.ppermute(raised.astype(jnp.bfloat16), 'grp', [(0, 1)])  9.14 us
    pallas_call x1, Pallas kernels, unite(): pl.pallas_call(unite_body, out_shape=jax.ShapeDtypeStruct((tokens, column...  6.75 us
    pallas_call x1, Pallas kernels, logits_of(): pl.pallas_call(logits_body, out_shape=jax.ShapeDtypeStruct((tokens, width...  6.25 us
  transfers between devices with their start and end apart: 2, of which 1 were waited for; matrix products, arithmetic and copies ran while one was open for 1% of the time, Pallas kernels for 27%

profile of v3, /device:TPU:0, one launch (start us, length us, event | category | flops | bytes accessed | tf_op | source)
XLA Modules:
  0.0 272.9 jit_solution(18220093264205819931)
XLA Ops:
  7.2 0.0 all-gather.2.cloned.1.call-start
  7.2 0.7 all-gather.2.cloned.1.call-update
  7.9 16.1 %shard_map.86.refs_0_ = bf16[3,2,1,64,1024]{4,3,2,1,0:T(8,128)(2,1)} custom-call(bf16[3,1,1,64,1024]{4,3,2,1,0:T(8,128)(2,1)} %bitcast.79), custom_call_target="tpu_custom_call" | custom-call | tf_op jit(solution)/shard_map/pallas_call | solution.py:98
  24.0 25.1 %shard_map.87 = bf16[3,2,2,64,1024]{4,3,2,1,0:T(8,128)(2,1)} custom-call(bf16[3,2,1,64,1024]{4,3,2,1,0:T(8,128)(2,1)} %shard_map.86.refs_0_), custom_call_target="tpu_custom_call" | custom-call | tf_op jit(solution)/shard_map/pallas_call | solution.py:98
  49.1 0.0 copy-start.2
  49.1 4.6 %copy-done.2 = bf16[3,1024,2048]{2,1,0:T(8,128)(2,1)S(1)} copy-done((bf16[3,1024,2048]{2,1,0:T(8,128)(2,1)S(1)}, bf16[3,1024,2048]{2,1,0:T(8,128)(2,1)}, u32[]{:S(2)}) %copy-start.2) | copy-done | bytes 12582936
  53.7 0.0 copy-start.3
  53.7 1.4 copy-done.3
  55.1 6.7 %shard_map.88 = bf16[256,2048]{1,0:T(8,128)(2,1)S(1)} custom-call(bf16[3,256,1024]{2,1,0:T(8,128)(2,1)S(1)} %bitcast.74, bf16[3,1024,2048]{2,1,0:T(8,128)(2,1)S(1)} %copy-done.2), custom_call_target="tpu_custom_call" | custom-call | tf_op jit(solution)/shard_map/pallas_call | solution.py:146
  61.8 0.0 copy-start.4
  61.8 1.0 copy-done.4
  62.8 0.0 copy-start.9
  62.8 26.4 %shard_map.89 = bf16[7,32,2048]{2,1,0:T(8,128)(2,1)} custom-call(bf16[8,32,2048]{2,1,0:T(8,128)(2,1)} %bitcast.75), custom_call_target="tpu_custom_call" | custom-call | tf_op jit(solution)/shard_map/pallas_call | solution.py:98
  89.2 0.0 copy-start.8
  89.2 1.5 fusion.11
  90.8 0.0 all-gather.2.cloned.1.call-done
  90.8 0.0 copy-start.7
  90.8 1.6 fusion.1
  92.4 0.7 fusion.15.refs_0_
  93.1 4.0 %shard_map.90 = f32[4,8,128]{2,1,0:T(8,128)} custom-call(f32[1,8,128]{2,1,0:T(8,128)} %fusion.15.refs_0_), custom_call_target="tpu_custom_call" | custom-call | tf_op jit(solution)/shard_map/pallas_call | solution.py:98
  97.1 0.7 reduce_sum.92
  97.8 0.1 add_rsqrt_fusion
  97.9 0.0 copy-done.9
  97.9 0.8 fusion.13.refs_0_
  98.7 27.4 %shard_map.91 = bf16[256,2048]{1,0:T(8,128)(2,1)} custom-call(bf16[32,2048]{1,0:T(8,128)(2,1)} %fusion.13.refs_0_), custom_call_target="tpu_custom_call" | custom-call | tf_op jit(solution)/shard_map/pallas_call | solution.py:98
  126.1 0.0 copy-done.8
  126.1 0.0 copy-done.7
  126.1 0.6 fusion.7.rows_ref
  126.7 0.0 copy-start.1
  126.7 5.6 %copy-done.1 = bf16[1,4000,2048]{2,1,0:T(8,128)(2,1)S(1)} copy-done((bf16[1,4000,2048]{2,1,0:T(8,128)(2,1)S(1)}, bf16[1,4000,2048]{2,1,0:T(8,128)(2,1)}, u32[]{:S(2)}) %copy-start.1) | copy-done | bytes 16384024
  132.4 6.3 %shard_map.92 = f32[256,4096]{1,0:T(8,128)S(1)} custom-call(bf16[256,2048]{1,0:T(8,128)(2,1)S(1)} %fusion.7.rows_ref, bf16[1,4000,2048]{2,1,0:T(8,128)(2,1)S(1)} %copy-done.1), custom_call_target="tpu_custom_call" | custom-call | tf_op jit(solution)/shard_map/pallas_call | solution.py:169
  138.6 0.0 copy-start
  138.6 2.0 copy-done
  140.7 4.7 %shard_map.93 = f32[2,1,64,4096]{3,2,1,0:T(8,128)} custom-call(f32[2,2,64,4096]{3,2,1,0:T(8,128)} %bitcast.72), custom_call_target="tpu_custom_call" | custom-call | tf_op jit(solution)/shard_map/pallas_call | solution.py:98
  145.3 3.8 %bitcast_add_fusion = f32[2,1,64,4096]{3,2,0,1:T(8,128)} fusion(f32[2,1,64,4096]{3,2,1,0:T(8,128)} %shard_map.93, f32[2,2,64,4096]{3,2,1,0:T(8,128)} %bitcast.73, s32[]{:T(128)S(6)} %select_n.79), kind=kLoop, calls=%fused_computation.8 | loop fusion | flops 524288 | bytes 6291460 | tf_op jit(solution)/shard_map/add | solution.py:222
  149.2 0.0 copy-start.5
  149.2 25.7 %shard_map.94 = f32[1,64,4096]{2,1,0:T(8,128)} custom-call(f32[2,64,4096]{2,1,0:T(8,128)} %bitcast.77), custom_call_target="tpu_custom_call" | custom-call | tf_op jit(solution)/shard_map/pallas_call | solution.py:98
  174.8 0.0 copy-done.5
  174.8 0.0 copy-start.10
  174.9 1.5 fusion.21
  176.3 0.2 fusion.8
  176.5 3.8 %collective-permute-start = (bf16[64,4096]{1,0:T(8,128)(2,1)S(1)}, bf16[64,4096]{1,0:T(8,128)(2,1)S(1)}, u32[]{:S(2)}, u32[]{:S(2)}) collective-permute-start(bf16[64,4096]{1,0:T(8,128)(2,1)S(1)} %fusion.8), channel_id=1, source_target_pairs={{0,16},{1,17},{2,18},{3,19},{4,20},{5,21},{6,22},{7,23},{8,24},{9,... | collective-permute-start | bytes 1572872 | tf_op jit(solution)/shard_map/ppermute | solution.py:229
  180.4 0.0 copy-done.10
  180.4 0.6 reduce_sum.98
  181.8 0.1 select_reduce_fusion
  181.9 9.1 %collective-permute-done = bf16[64,4096]{1,0:T(8,128)(2,1)S(1)} collective-permute-done((bf16[64,4096]{1,0:T(8,128)(2,1)S(1)}, bf16[64,4096]{1,0:T(8,128)(2,1)S(1)}, u32[]{:S(2)}, u32[]{:S(2)}) %collective-permute-start) | collective-permute-done | bytes 524320 | tf_op jit(solution)/shard_map/ppermute | solution.py:229
  191.0 0.5 fusion.9
  191.5 0.7 fusion.14.refs_0_
  192.2 10.6 %shard_map.95 = f32[8,8,128]{2,1,0:T(8,128)} custom-call(f32[1,8,128]{2,1,0:T(8,128)} %fusion.14.refs_0_), custom_call_target="tpu_custom_call" | custom-call | tf_op jit(solution)/shard_map/pallas_call | solution.py:98
  202.8 0.8 reshape.127
  203.6 0.1 reshape.128
  203.8 0.5 fusion.20
  204.3 1.1 fusion.10.refs_0_
  205.5 0.0 copy-start.6
  205.5 17.6 %shard_map.96.refs_0_ = bf16[1,2,1,64,4096]{4,3,2,1,0:T(8,128)(2,1)} custom-call(bf16[1,1,1,64,4096]{4,3,2,1,0:T(8,128)(2,1)} %fusion.10.refs_0_), custom_call_target="tpu_custom_call" | custom-call | tf_op jit(solution)/shard_map/pallas_call | solution.py:98
  223.0 33.0 %shard_map.97 = bf16[1,2,2,64,4096]{4,3,2,1,0:T(8,128)(2,1)} custom-call(bf16[1,2,1,64,4096]{4,3,2,1,0:T(8,128)(2,1)} %shard_map.96.refs_0_), custom_call_target="tpu_custom_call" | custom-call | tf_op jit(solution)/shard_map/pallas_call | solution.py:98
  256.1 0.0 copy-done.6
  256.1 10.0 %fusion = bf16[1,4000,2048]{2,1,0:T(8,128)(2,1)} fusion(f32[]{:T(128)S(6)} %select_n.75, bf16[256,2048]{1,0:T(8,128)(2,1)S(1)} %copy-done.6, bf16[1,256,4096]{2,1,0:T(8,128)(2,1)} %bitcast.78), kind=kOutput, calls=%fused_computation.1 | convolution fusion | flops 4210688000 | bytes 19529732 | tf_op jit(solution)/shard_map/tv,td->vd/dot_general | solution.py:262
  (14 shorter events, 0.2 us)
Async XLA Ops:
  7.2 83.6 %all-gather.2.cloned.1.call-start = ((), (), s32[]{:S(2)}) async-start(), calls=%async_computation | async-start | bytes 1310720 | tf_op jit(solution)/shard_map/all_gather | solution.py:195
  49.1 4.6 %copy-start.2 = (bf16[3,1024,2048]{2,1,0:T(8,128)(2,1)S(1)}, bf16[3,1024,2048]{2,1,0:T(8,128)(2,1)}, u32[]{:S(2)}) copy-start(bf16[3,1024,2048]{2,1,0:T(8,128)(2,1)} %weight_ref.1) | copy-start | bytes 37748740
  53.7 1.4 copy-start.3
  61.8 1.0 copy-start.4
  62.8 35.1 %copy-start.9 = (f32[2048]{0:T(1024)S(1)}, f32[2048]{0:T(1024)}, u32[]{:S(2)}) copy-start(f32[2048]{0:T(1024)} %param.12) | copy-start | bytes 24580
  89.2 36.9 %copy-start.8 = (f32[2048]{0:T(1024)S(1)}, f32[2048]{0:T(1024)}, u32[]{:S(2)}) copy-start(f32[2048]{0:T(1024)} %param.11) | copy-start | bytes 24580
  90.8 35.3 %copy-start.7 = (bf16[256,2048]{1,0:T(8,128)(2,1)S(1)}, bf16[256,2048]{1,0:T(8,128)(2,1)}, u32[]{:S(2)}) copy-start(bf16[256,2048]{1,0:T(8,128)(2,1)} %all-gather.2.cloned.1.call-done) | copy-start | bytes 3145732
  126.7 5.7 %copy-start.1 = (bf16[1,4000,2048]{2,1,0:T(8,128)(2,1)S(1)}, bf16[1,4000,2048]{2,1,0:T(8,128)(2,1)}, u32[]{:S(2)}) copy-start(bf16[1,4000,2048]{2,1,0:T(8,128)(2,1)} %head_ref.1) | copy-start | bytes 49152004
  138.6 2.0 copy-start
  149.2 25.7 %copy-start.5 = (f32[2,1,64,4096]{3,2,0,1:T(8,128)S(1)}, f32[2,1,64,4096]{3,2,0,1:T(8,128)}, u32[]{:S(2)}) copy-start(f32[2,1,64,4096]{3,2,0,1:T(8,128)} %bitcast_add_fusion) | copy-start | bytes 6291460
  174.8 5.6 %copy-start.10 = (s32[4]{0:T(128)S(1)}, s32[4]{0:T(128)}, u32[]{:S(2)}) copy-start(s32[4]{0:T(128)} %param.13) | copy-start | bytes 52
  176.5 14.5 %collective-permute-start = (bf16[64,4096]{1,0:T(8,128)(2,1)S(1)}, bf16[64,4096]{1,0:T(8,128)(2,1)S(1)}, u32[]{:S(2)}, u32[]{:S(2)}) collective-permute-start(bf16[64,4096]{1,0:T(8,128)(2,1)S(1)} %fusion.8), channel_id=1, source_target_pairs={{0,16},{1,17},{2,18},{3,19},{4,20},{5,21},{6,22},{7,23},{8,24},{9,... | collective-permute-start | bytes 1572872 | tf_op jit(solution)/shard_map/ppermute | solution.py:229
  205.5 50.6 %copy-start.6 = (bf16[256,2048]{1,0:T(8,128)(2,1)S(1)}, bf16[256,2048]{1,0:T(8,128)(2,1)}, u32[]{:S(2)}) copy-start(bf16[256,2048]{1,0:T(8,128)(2,1)} %shard_map.91) | copy-start | bytes 3145732
Sparse Core Ops, SparseCore 0:
  9.6 30.6 all-gather.1

commit v4 on v3

--- a/solution.py
+++ b/solution.py
@@ -41,7 +41,8 @@
 def exchange_body(items, *refs):
     count = len(items)
     ins, outs = refs[:count], refs[count : 2 * count]
-    local_sem, send_sem, recv_sem = refs[2 * count :]
+    local_sem, send_sem, recv_sem = refs[2 * count : 2 * count + 3]
+    held = refs[2 * count + 3 :]
     groups = [item[0]() for item in items]
     barrier = pltpu.get_barrier_semaphore()
     total = 0
@@ -77,8 +78,11 @@
                 copies.append(copy)
                 slot += 1
         if kind == "gather":
+            taken = pltpu.make_async_copy(source, held[number], local_sem.at[number])
+            taken.start()
+            taken.wait()
             own = pltpu.make_async_copy(
-                source, window(target, dim, me, source.shape[dim]), local_sem.at[number]
+                held[number], window(target, dim, me, source.shape[dim]), local_sem.at[number]
             )
             own.start()
             copies.append(own)
@@ -104,6 +108,10 @@
             pltpu.SemaphoreType.DMA((len(arrays),)),
             pltpu.SemaphoreType.DMA((slots,)),
             pltpu.SemaphoreType.DMA((slots,)),
+        ]
+        + [
+            pltpu.VMEM(array.shape if item[1] == "gather" else (8, 128), array.dtype)
+            for array, item in zip(arrays, items)
         ],
         compiler_params=pltpu.CompilerParams(collective_id=number, has_side_effects=True),
     )(*arrays)

time: 273 us -> 212 us (0.78)
  Pallas kernels: 203 us -> 141 us
    pallas_call x10, Pallas kernels: 190 us -> 128 us  [exchange(): pl.pallas_call(functools.partial(exchange_body, items), out_shape=shapes,...]
  transfers between devices with their start and end apart: 2 -> 2, of which waited for: 1 -> 1; matrix products, arithmetic and copies ran while one was open for 1% -> 1% of each run, Pallas kernels for 27% -> 23%
where the time goes in v4:
time: 212 us; the launch traced here: 211 us
  Pallas kernels  141 us (67%)
  local copies, waits for them, and re-layouts  15.6 us (7%)
  other arithmetic  15.2 us (7%)
  between operations  15.1 us (7%)
  matrix products  9.98 us (5%)
  waiting for transfers between devices  9.84 us (5%)
  starting transfers between devices  3.86 us (2%)
    pallas_call x10, Pallas kernels, exchange(): pl.pallas_call(functools.partial(exchange_body, items), out_shape=shapes,...  128 us
    unnamed x22, local copies, waits for them, and re-layouts  14.7 us
    dot_general x1, matrix products, per_device(): jnp.einsum('tv,td->vd', all_weighted, draft_rows, preferred_element_type=...  9.98 us
    ppermute x1, waiting for transfers between devices, per_device(): lax.ppermute(raised.astype(jnp.bfloat16), 'grp', [(0, 1)])  9.14 us
    pallas_call x1, Pallas kernels, unite(): pl.pallas_call(unite_body, out_shape=jax.ShapeDtypeStruct((tokens, column...  6.75 us
    pallas_call x1, Pallas kernels, logits_of(): pl.pallas_call(logits_body, out_shape=jax.ShapeDtypeStruct((tokens, width...  6.25 us
  transfers between devices with their start and end apart: 2, of which 1 were waited for; matrix products, arithmetic and copies ran while one was open for 1% of the time, Pallas kernels for 23%

profile of v4, /device:TPU:0, one launch (start us, length us, event | category | flops | bytes accessed | tf_op | source)
XLA Modules:
  0.0 210.9 jit_solution(15556175930584401394)
XLA Ops:
  7.2 0.0 all-gather.2.cloned.1.call-start
  7.2 0.7 all-gather.2.cloned.1.call-update
  7.9 12.5 %shard_map.86.refs_0_ = bf16[3,2,1,64,1024]{4,3,2,1,0:T(8,128)(2,1)} custom-call(bf16[3,1,1,64,1024]{4,3,2,1,0:T(8,128)(2,1)} %bitcast.79), custom_call_target="tpu_custom_call" | custom-call | tf_op jit(solution)/shard_map/pallas_call | solution.py:102
  20.4 2.7 %shard_map.87 = bf16[3,2,2,64,1024]{4,3,2,1,0:T(8,128)(2,1)} custom-call(bf16[3,2,1,64,1024]{4,3,2,1,0:T(8,128)(2,1)} %shard_map.86.refs_0_), custom_call_target="tpu_custom_call" | custom-call | tf_op jit(solution)/shard_map/pallas_call | solution.py:102
  23.2 0.0 copy-start.2
  23.2 4.6 %copy-done.2 = bf16[3,1024,2048]{2,1,0:T(8,128)(2,1)S(1)} copy-done((bf16[3,1024,2048]{2,1,0:T(8,128)(2,1)S(1)}, bf16[3,1024,2048]{2,1,0:T(8,128)(2,1)}, u32[]{:S(2)}) %copy-start.2) | copy-done | bytes 12582936
  27.8 0.0 copy-start.3
  27.8 1.4 copy-done.3
  29.2 6.7 %shard_map.88 = bf16[256,2048]{1,0:T(8,128)(2,1)S(1)} custom-call(bf16[3,256,1024]{2,1,0:T(8,128)(2,1)S(1)} %bitcast.74, bf16[3,1024,2048]{2,1,0:T(8,128)(2,1)S(1)} %copy-done.2), custom_call_target="tpu_custom_call" | custom-call | tf_op jit(solution)/shard_map/pallas_call | solution.py:154
  35.9 0.0 copy-start.4
  36.0 1.0 copy-done.4
  36.9 0.0 copy-start.9
  36.9 26.3 %shard_map.89 = bf16[7,32,2048]{2,1,0:T(8,128)(2,1)} custom-call(bf16[8,32,2048]{2,1,0:T(8,128)(2,1)} %bitcast.75), custom_call_target="tpu_custom_call" | custom-call | tf_op jit(solution)/shard_map/pallas_call | solution.py:102
  63.3 0.0 copy-start.8
  63.3 1.5 fusion.11
  64.8 0.0 all-gather.2.cloned.1.call-done
  64.9 0.0 copy-start.7
  64.9 1.6 fusion.1
  66.5 0.7 fusion.15.refs_0_
  67.1 4.0 %shard_map.90 = f32[4,8,128]{2,1,0:T(8,128)} custom-call(f32[1,8,128]{2,1,0:T(8,128)} %fusion.15.refs_0_), custom_call_target="tpu_custom_call" | custom-call | tf_op jit(solution)/shard_map/pallas_call | solution.py:102
  71.1 0.7 reduce_sum.92
  71.9 0.1 add_rsqrt_fusion
  72.0 0.0 copy-done.9
  72.0 0.8 fusion.13.refs_0_
  72.7 27.4 %shard_map.91 = bf16[256,2048]{1,0:T(8,128)(2,1)} custom-call(bf16[32,2048]{1,0:T(8,128)(2,1)} %fusion.13.refs_0_), custom_call_target="tpu_custom_call" | custom-call | tf_op jit(solution)/shard_map/pallas_call | solution.py:102
  100.1 0.0 copy-done.8
  100.2 0.0 copy-done.7
  100.2 0.6 fusion.7.rows_ref
  100.8 0.0 copy-start.1
  100.8 5.6 %copy-done.1 = bf16[1,4000,2048]{2,1,0:T(8,128)(2,1)S(1)} copy-done((bf16[1,4000,2048]{2,1,0:T(8,128)(2,1)S(1)}, bf16[1,4000,2048]{2,1,0:T(8,128)(2,1)}, u32[]{:S(2)}) %copy-start.1) | copy-done | bytes 16384024
  106.4 6.3 %shard_map.92 = f32[256,4096]{1,0:T(8,128)S(1)} custom-call(bf16[256,2048]{1,0:T(8,128)(2,1)S(1)} %fusion.7.rows_ref, bf16[1,4000,2048]{2,1,0:T(8,128)(2,1)S(1)} %copy-done.1), custom_call_target="tpu_custom_call" | custom-call | tf_op jit(solution)/shard_map/pallas_call | solution.py:177
  112.7 0.0 copy-start
  112.7 2.0 copy-done
  114.7 4.7 %shard_map.93 = f32[2,1,64,4096]{3,2,1,0:T(8,128)} custom-call(f32[2,2,64,4096]{3,2,1,0:T(8,128)} %bitcast.72), custom_call_target="tpu_custom_call" | custom-call | tf_op jit(solution)/shard_map/pallas_call | solution.py:102
  119.4 3.8 %bitcast_add_fusion = f32[2,1,64,4096]{3,2,0,1:T(8,128)} fusion(f32[2,1,64,4096]{3,2,1,0:T(8,128)} %shard_map.93, f32[2,2,64,4096]{3,2,1,0:T(8,128)} %bitcast.73, s32[]{:T(128)S(6)} %select_n.79), kind=kLoop, calls=%fused_computation.8 | loop fusion | flops 524288 | bytes 6291460 | tf_op jit(solution)/shard_map/add | solution.py:230
  123.2 0.0 copy-start.5
  123.2 25.7 %shard_map.94 = f32[1,64,4096]{2,1,0:T(8,128)} custom-call(f32[2,64,4096]{2,1,0:T(8,128)} %bitcast.77), custom_call_target="tpu_custom_call" | custom-call | tf_op jit(solution)/shard_map/pallas_call | solution.py:102
  148.9 0.0 copy-done.5
  148.9 0.0 copy-start.10
  148.9 1.5 fusion.21
  150.4 0.2 fusion.8
  150.6 3.8 %collective-permute-start = (bf16[64,4096]{1,0:T(8,128)(2,1)S(1)}, bf16[64,4096]{1,0:T(8,128)(2,1)S(1)}, u32[]{:S(2)}, u32[]{:S(2)}) collective-permute-start(bf16[64,4096]{1,0:T(8,128)(2,1)S(1)} %fusion.8), channel_id=1, source_target_pairs={{0,16},{1,17},{2,18},{3,19},{4,20},{5,21},{6,22},{7,23},{8,24},{9,... | collective-permute-start | bytes 1572872 | tf_op jit(solution)/shard_map/ppermute | solution.py:237
  154.4 0.0 copy-done.10
  154.4 0.6 reduce_sum.98
  155.8 0.1 select_reduce_fusion
  155.9 9.1 %collective-permute-done = bf16[64,4096]{1,0:T(8,128)(2,1)S(1)} collective-permute-done((bf16[64,4096]{1,0:T(8,128)(2,1)S(1)}, bf16[64,4096]{1,0:T(8,128)(2,1)S(1)}, u32[]{:S(2)}, u32[]{:S(2)}) %collective-permute-start) | collective-permute-done | bytes 524320 | tf_op jit(solution)/shard_map/ppermute | solution.py:237
  165.0 0.5 fusion.9
  165.6 0.7 fusion.14.refs_0_
  166.2 10.6 %shard_map.95 = f32[8,8,128]{2,1,0:T(8,128)} custom-call(f32[1,8,128]{2,1,0:T(8,128)} %fusion.14.refs_0_), custom_call_target="tpu_custom_call" | custom-call | tf_op jit(solution)/shard_map/pallas_call | solution.py:102
  176.8 0.8 reshape.127
  177.6 0.1 reshape.128
  177.9 0.5 fusion.20
  178.4 1.1 fusion.10.refs_0_
  179.5 0.0 copy-start.6
  179.5 11.5 %shard_map.96.refs_0_ = bf16[1,2,1,64,4096]{4,3,2,1,0:T(8,128)(2,1)} custom-call(bf16[1,1,1,64,4096]{4,3,2,1,0:T(8,128)(2,1)} %fusion.10.refs_0_), custom_call_target="tpu_custom_call" | custom-call | tf_op jit(solution)/shard_map/pallas_call | solution.py:102
  191.0 3.1 %shard_map.97 = bf16[1,2,2,64,4096]{4,3,2,1,0:T(8,128)(2,1)} custom-call(bf16[1,2,1,64,4096]{4,3,2,1,0:T(8,128)(2,1)} %shard_map.96.refs_0_), custom_call_target="tpu_custom_call" | custom-call | tf_op jit(solution)/shard_map/pallas_call | solution.py:102
  194.1 0.0 copy-done.6
  194.1 10.0 %fusion = bf16[1,4000,2048]{2,1,0:T(8,128)(2,1)} fusion(f32[]{:T(128)S(6)} %select_n.75, bf16[256,2048]{1,0:T(8,128)(2,1)S(1)} %copy-done.6, bf16[1,256,4096]{2,1,0:T(8,128)(2,1)} %bitcast.78), kind=kOutput, calls=%fused_computation.1 | convolution fusion | flops 4210688000 | bytes 19529732 | tf_op jit(solution)/shard_map/tv,td->vd/dot_general | solution.py:270
  (14 shorter events, 0.2 us)
Async XLA Ops:
  7.2 57.7 %all-gather.2.cloned.1.call-start = ((), (), s32[]{:S(2)}) async-start(), calls=%async_computation | async-start | bytes 1310720 | tf_op jit(solution)/shard_map/all_gather | solution.py:203
  23.2 4.6 %copy-start.2 = (bf16[3,1024,2048]{2,1,0:T(8,128)(2,1)S(1)}, bf16[3,1024,2048]{2,1,0:T(8,128)(2,1)}, u32[]{:S(2)}) copy-start(bf16[3,1024,2048]{2,1,0:T(8,128)(2,1)} %weight_ref.1) | copy-start | bytes 37748740
  27.8 1.4 copy-start.3
  35.9 1.0 copy-start.4
  36.9 35.0 %copy-start.9 = (f32[2048]{0:T(1024)S(1)}, f32[2048]{0:T(1024)}, u32[]{:S(2)}) copy-start(f32[2048]{0:T(1024)} %param.12) | copy-start | bytes 24580
  63.3 36.9 %copy-start.8 = (f32[2048]{0:T(1024)S(1)}, f32[2048]{0:T(1024)}, u32[]{:S(2)}) copy-start(f32[2048]{0:T(1024)} %param.11) | copy-start | bytes 24580
  64.9 35.3 %copy-start.7 = (bf16[256,2048]{1,0:T(8,128)(2,1)S(1)}, bf16[256,2048]{1,0:T(8,128)(2,1)}, u32[]{:S(2)}) copy-start(bf16[256,2048]{1,0:T(8,128)(2,1)} %all-gather.2.cloned.1.call-done) | copy-start | bytes 3145732
  100.8 5.7 %copy-start.1 = (bf16[1,4000,2048]{2,1,0:T(8,128)(2,1)S(1)}, bf16[1,4000,2048]{2,1,0:T(8,128)(2,1)}, u32[]{:S(2)}) copy-start(bf16[1,4000,2048]{2,1,0:T(8,128)(2,1)} %head_ref.1) | copy-start | bytes 49152004
  112.7 2.0 copy-start
  123.2 25.7 %copy-start.5 = (f32[2,1,64,4096]{3,2,0,1:T(8,128)S(1)}, f32[2,1,64,4096]{3,2,0,1:T(8,128)}, u32[]{:S(2)}) copy-start(f32[2,1,64,4096]{3,2,0,1:T(8,128)} %bitcast_add_fusion) | copy-start | bytes 6291460
  148.9 5.5 %copy-start.10 = (s32[4]{0:T(128)S(1)}, s32[4]{0:T(128)}, u32[]{:S(2)}) copy-start(s32[4]{0:T(128)} %param.13) | copy-start | bytes 52
  150.6 14.4 %collective-permute-start = (bf16[64,4096]{1,0:T(8,128)(2,1)S(1)}, bf16[64,4096]{1,0:T(8,128)(2,1)S(1)}, u32[]{:S(2)}, u32[]{:S(2)}) collective-permute-start(bf16[64,4096]{1,0:T(8,128)(2,1)S(1)} %fusion.8), channel_id=1, source_target_pairs={{0,16},{1,17},{2,18},{3,19},{4,20},{5,21},{6,22},{7,23},{8,24},{9,... | collective-permute-start | bytes 1572872 | tf_op jit(solution)/shard_map/ppermute | solution.py:237
  179.5 14.6 %copy-start.6 = (bf16[256,2048]{1,0:T(8,128)(2,1)S(1)}, bf16[256,2048]{1,0:T(8,128)(2,1)}, u32[]{:S(2)}) copy-start(bf16[256,2048]{1,0:T(8,128)(2,1)} %shard_map.91) | copy-start | bytes 3145732
Sparse Core Ops, SparseCore 0:
  9.6 30.6 all-gather.1
